TPU v7x, 128 devices: a whole 4x4x4 slice. The times are simulated.
128 devices in a mesh: seq: 16 (over z, y), head: 8 (over x, core).
Axes of the slice: x: 4, y: 4, z: 4, core: 2. Of those that a mesh axis runs over, the one named last changes fastest.
Arguments:
- latents: bfloat16 [2048, 2048], replicated, may hold values from -120 to 120
- context: bfloat16 [16384, 2048], P('seq'), may hold values from -6 to 6
- offsets: int32 [2048], replicated, may hold values from 14336 to 16383, as said below
- w_query: bfloat16 [2048, 2048], P(None, 'head'), may hold values from -1 to 1
- w_key: bfloat16 [2048, 2048], P(None, 'head'), may hold values from -1 to 1
- w_value: bfloat16 [2048, 2048], P(None, 'head'), may hold values from -0.125 to 0.125
- grad_out: bfloat16 [2048, 2048], P(None, 'head'), may hold values from -6 to 6
Outputs:
- attention_out: bfloat16 [2048, 2048], P('seq', 'head')
- grad_latents: bfloat16 [2048, 2048], P('seq', 'head')
- grad_context: bfloat16 [16384, 2048], P('seq', 'head')
Inputs may be any that keep to these rules, and one draw needn't show every extreme that they name: Latent query i sees context positions 0 through offsets[i]; the latents are causal: offsets[i] = min(s + i, 16383) for one shift s of the draw, so the latents' own span ends at or runs past the stretch's last position and latents past it see the whole stretch.
All inputs are finite; a program needn't handle non-finite values.
Results may differ from a plain program's by a relative error of at most 0.028.
Values may be sent and summed in bfloat16 or wider, within the bound.
A program may use at most 128 MiB of HBM per device.

v0:
```python
import jax
import jax.numpy as jnp
from jax import lax
from jax.sharding import PartitionSpec as P

E = 128


masked_floor = -1e30


def body(latents, context, offsets, w_query, w_key, w_value, grad_out):
    scaling = E ** (-0.5)
    tokens_here = context.shape[0]
    latent_rows = latents.shape[0]
    columns = w_query.shape[1]
    groups = columns // E
    query_rows = jnp.dot(latents, w_query, preferred_element_type=jnp.float32).astype(jnp.bfloat16)
    key_rows = jnp.dot(context, w_key, preferred_element_type=jnp.float32).astype(jnp.bfloat16)
    value_rows = jnp.dot(context, w_value, preferred_element_type=jnp.float32).astype(jnp.bfloat16)
    positions = lax.axis_index("seq") * tokens_here + jnp.arange(tokens_here, dtype=jnp.int32)
    visible = (positions[None, :] <= offsets[:, None])[:, None, :]
    query_heads = query_rows.reshape(latent_rows, groups, E)
    key_heads = key_rows.reshape(tokens_here, groups, E)
    value_heads = value_rows.reshape(tokens_here, groups, E)
    scores = (
        jnp.einsum("ihe,jhe->ihj", query_heads, key_heads, preferred_element_type=jnp.float32)
        * scaling
    )
    local_max = jnp.max(jnp.where(visible, scores, masked_floor), axis=2)
    weights = jnp.where(visible, jnp.exp(scores - local_max[:, :, None]), 0.0)
    local_sum = jnp.sum(weights, axis=2)
    local_out = jnp.einsum(
        "ihj,jhe->ihe",
        weights.astype(jnp.bfloat16),
        value_heads,
        preferred_element_type=jnp.float32,
    )
    row_block = latent_rows // lax.axis_size("seq")
    row_start = lax.axis_index("seq") * row_block
    highest = lax.pmax(local_max, "seq")
    factor = jnp.exp(local_max - highest)
    scaled_out = (local_out * factor[:, :, None]).reshape(latent_rows, columns)
    totals, merged = lax.psum((local_sum * factor, scaled_out), "seq")
    attention3 = merged.reshape(latent_rows, groups, E) / totals[:, :, None]
    attention = attention3.astype(jnp.bfloat16).reshape(latent_rows, columns)
    log_total = highest + jnp.log(totals)
    products = grad_out.astype(jnp.float32) * attention.astype(jnp.float32)
    row_delta = jnp.sum(products.reshape(latent_rows, groups, E), axis=2)
    attention_block = lax.dynamic_slice_in_dim(attention, row_start, row_block, 0)
    grad_heads = grad_out.reshape(latent_rows, groups, E)
    probabilities = jnp.where(visible, jnp.exp(scores - log_total[:, :, None]), 0.0)
    grad_values = jnp.einsum(
        "ihj,ihe->jhe",
        probabilities.astype(jnp.bfloat16),
        grad_heads,
        preferred_element_type=jnp.float32,
    )
    grad_values = grad_values.astype(jnp.bfloat16).reshape(tokens_here, columns)
    grad_probs = jnp.einsum(
        "ihe,jhe->ihj", grad_heads, value_heads, preferred_element_type=jnp.float32
    )
    grad_scores = (probabilities * (grad_probs - row_delta[:, :, None])).astype(jnp.bfloat16)
    grad_query = (
        jnp.einsum(
            "ihj,jhe->ihe", grad_scores, key_heads, preferred_element_type=jnp.float32
        ).reshape(latent_rows, columns)
        * scaling
    )
    grad_keys = (
        jnp.einsum("ihj,ihe->jhe", grad_scores, query_heads, preferred_element_type=jnp.float32)
        * scaling
    )
    grad_keys = grad_keys.astype(jnp.bfloat16).reshape(tokens_here, columns)
    query_share = lax.psum_scatter(
        grad_query.astype(jnp.bfloat16), "seq", scatter_dimension=0, tiled=True
    )
    latent_term = jnp.dot(query_share, w_query.T, preferred_element_type=jnp.float32)
    grad_latents = lax.psum_scatter(
        latent_term.astype(jnp.bfloat16), "head", scatter_dimension=1, tiled=True
    )
    context_term = jnp.dot(grad_keys, w_key.T, preferred_element_type=jnp.float32)
    context_term = context_term + jnp.dot(
        grad_values, w_value.T, preferred_element_type=jnp.float32
    )
    grad_context = lax.psum_scatter(
        context_term.astype(jnp.bfloat16), "head", scatter_dimension=1, tiled=True
    )
    return (attention_block, grad_latents, grad_context)


def solution(mesh):
    placed = (
        P(),
        P("seq", None),
        P(),
        P(None, "head"),
        P(None, "head"),
        P(None, "head"),
        P(None, "head"),
    )
    return jax.shard_map(
        body,
        mesh=mesh,
        in_specs=placed,
        out_specs=(P("seq", "head"), P("seq", "head"), P("seq", "head")),
        check_vma=False,
    )
```

profile of v0, /device:TPU:0, one launch (start us, length us, event | category | flops | bytes accessed | tf_op | source)
XLA Modules:
  0.0 396.2 jit_solution(18237532535886096471)
XLA Ops:
  7.2 0.0 copy-start
  7.2 0.0 all-reduce.2.cloned.1.call-start
  7.2 0.0 copy-start.16
  7.3 0.0 slice-start
  7.3 4.7 %convolution_convert_fusion.3 = bf16[1024,256]{0,1:T(8,128)(2,1)} fusion(bf16[1024,2048]{1,0:T(8,128)(2,1)} %param.8, bf16[2048,256]{1,0:T(8,128)(2,1)} %param.12), kind=kOutput, calls=%fused_computation.32 | convolution fusion | flops 1074003968 | bytes 5767168 | tf_op jit(solution)/shard_map/dot_general | solution.py:20
  12.0 0.0 copy-done
  12.0 0.0 copy-done.16
  12.0 0.0 copy-start.10
  12.0 0.0 slice-start.1
  12.0 1.3 convolution_convert_fusion.2
  13.3 0.0 copy-done.15
  13.3 0.0 copy-start.5
  13.4 1.5 broadcast_compare_fusion
  14.8 0.0 slice-done
  14.8 0.0 copy-done.10
  14.9 0.0 slice-done.1
  14.9 2.4 convolution_convert_fusion
  17.3 0.0 copy-start.8
  17.3 0.0 copy-done.5
  17.3 0.0 copy-done.3
  17.3 7.7 %fusion.2 = (f32[2048,2]{0,1:T(2,128)S(1)}, f32[2,1024,2048]{2,1,0:T(8,128)}) fusion(pred[2048,1024]{0,1:T(8,128)(4,1)S(1)} %broadcast_compare_fusion, bf16[1024,2,128]{0,2,1:T(8,128)(2,1)S(1)} %bitcast.85, bf16[2048,2,128]{0,2,1:T(8,128)(2,1)S(1)} %bitcast.89), kind=kOutput, calls=%fused_computation.6 | convolution fusion | flops 1086320640 | bytes 20463616 | tf_op jit(solution)/shard_map/ihe,jhe->ihj/dot_general | solution.py:27
  25.0 0.0 copy-done.8
  25.0 0.0 copy-start.11
  25.0 76.0 %pmax.7 = f32[2048,2]{0,1:T(2,128)} all-reduce(f32[2048,2]{0,1:T(2,128)S(1)} %get-tuple-element.7), channel_id=1, replica_groups=mesh['seq'=16,'head'=8] {'seq'}, use_global_device_ids=true, to_apply=%region_1.2 | all-reduce | flops 4096 | bytes 32768 | tf_op jit(solution)/shard_map/pmax | solution.py:41
  101.0 0.0 copy-done.11
  101.0 8.4 %fusion.8 = f32[2048,2]{0,1:T(2,128)S(1)} fusion(f32[2,1024,2048]{2,1,0:T(8,128)} %get-tuple-element.8, f32[2048,2]{0,1:T(2,128)} %copy-done.11, pred[2048,1024]{0,1:T(8,128)(4,1)} %copy-done.3), kind=kLoop, calls=%fused_computation.12 | loop fusion | flops 16773120 | bytes 18907136 | tf_op jit(solution)/shard_map/reduce_sum | solution.py:32
  109.4 0.0 copy-done.12
  109.4 0.0 copy-done.13
  109.5 0.6 fusion.33
  110.1 2.4 copy-done.2
  112.4 7.3 %fusion.19 = f32[2048,2,128]{0,2,1:T(8,128)} fusion(bf16[1024,2,128]{0,2,1:T(8,128)(2,1)} %bitcast.96, f32[2,1024,2048]{2,1,0:T(8,128)S(1)} %copy-done.2, f32[2048,2]{0,1:T(2,128)} %copy-done.11, pred[2048,1024]{0,1:T(8,128)(4,1)} %copy-done.3, f32[2048,2]{0,1:T(2,128)} %get-tuple-element.6), kind=kOutput, calls=%fused_computation.22 | convolution fusion | flops 1091043328 | bytes 21528576 | tf_op jit(solution)/shard_map/ihj,jhe->ihe/dot_general | solution.py:33
  119.7 2.9 copy.24
  122.6 0.0 all-reduce.2.cloned.1.call-update
  122.7 0.0 reduce-scatter.10.cloned.1.call-start
  122.7 70.0 %psum.15 = f32[2048,2]{0,1:T(2,128)S(1)} all-reduce(f32[2048,2]{0,1:T(2,128)} %get-tuple-element.5), channel_id=1, replica_groups=mesh['seq'=16,'head'=8] {'seq'}, use_global_device_ids=true, to_apply=%region_4.5 | all-reduce | flops 4096 | bytes 32768 | tf_op jit(solution)/shard_map/psum | solution.py:44
  192.7 0.4 copy.25
  193.1 2.3 copy.42
  195.4 0.0 copy-done.14
  195.4 14.2 %all-reduce.2.cloned.1.call-done = f32[2048,256]{1,0:T(8,128)} async-done(((f32[2048,256]{1,0:T(8,128)}), f32[2048,256]{1,0:T(8,128)}) %all-reduce.2.cloned.1.call-update) | async-done | bytes 2097168 | tf_op jit(solution)/shard_map/psum | solution.py:44
  209.6 4.6 %div.11 = f32[2048,2,128]{2,1,0:T(2,128)S(1)} broadcast(f32[2048,2]{1,0:T(8,128)S(1)} %copy.25), dimensions={0,1} | broadcast | bytes 2113536 | tf_op jit(solution)/shard_map/div | solution.py:45
  214.2 0.0 copy-start.4
  214.2 4.2 %convert_multiply_fusion = (f32[2048,256]{1,0:T(8,128)}, bf16[2048,256]{1,0:T(8,128)(2,1)}) fusion(bf16[2048,256]{1,0:T(8,128)(2,1)} %param.13, f32[2048,256]{1,0:T(8,128)} %all-reduce.2.cloned.1.call-done, f32[256,8,2,128]{3,2,1,0:T(2,128)S(1)} %bitcast.84), kind=kLoop, calls=%fused_computation.28 | loop fusion | flops 2621440 | bytes 8388608 | tf_op jit(solution)/shard_map/mul | solution.py:48
  218.4 3.3 reshape.74
  221.7 5.6 %reduce_sum.19 = f32[2048,2]{1,0:T(8,128)} reduce(f32[2048,2,128]{2,1,0:T(2,128)} %reshape.74, f32[]{:T(128)} %constant.6.clone.1), dimensions={2}, to_apply=%region_5.6 | reduce | flops 520192 | bytes 2113540 | tf_op jit(solution)/shard_map/reduce_sum | solution.py:49
  227.4 1.6 copy.28
  228.9 9.6 %fusion.1 = bf16[2048,2,1024]{0,2,1:T(8,128)(2,1)S(1)} fusion(f32[2,1024,2048]{2,1,0:T(8,128)} %get-tuple-element.8, f32[2048,2]{0,1:T(2,128)S(1)} %copy.28, f32[2048,2]{0,1:T(2,128)S(1)} %log_add_fusion, pred[2048,1024]{0,1:T(8,128)(4,1)S(1)} %copy-done.4, bf16[1024,2,128]{0,2,1:T(8,128)(2,1)} %bitcast.97, bf16[2048,2,128]{0,2,1:T(8,128)(2,1)} %bitcast.91), kind=kOutput, calls=%fused_computation.2 | convolution fusion | flops 1098907648 | bytes 28868608 | tf_op jit(solution)/shard_map/ihe,jhe->ihj/dot_general | solution.py:60
  238.5 3.2 copy-done.1
  241.7 1.3 fusion.22
  243.0 1.3 copy.40
  244.3 0.0 reduce-scatter.10.cloned.1.call-update
  244.3 0.3 reduce-scatter.6.cloned.1.call-start
  244.6 9.0 %fusion.25 = bf16[2,1024,128]{1,2,0:T(8,128)(2,1)S(1)} fusion(bf16[2048,2,128]{0,2,1:T(8,128)(2,1)} %bitcast.92, f32[2,1024,2048]{2,1,0:T(8,128)} %get-tuple-element.8, f32[2048,2]{0,1:T(2,128)S(1)} %log_add_fusion, pred[2048,1024]{0,1:T(8,128)(4,1)} %copy-done.3), kind=kOutput, calls=%fused_computation.33 | convolution fusion | flops 1090781184 | bytes 20463616 | tf_op jit(solution)/shard_map/ihj,ihe->jhe/dot_general | solution.py:53
  253.6 6.3 %fusion.24 = bf16[2,128,1024]{2,1,0:T(8,128)(2,1)S(1)} fusion(bf16[2048,2,128]{0,2,1:T(8,128)(2,1)S(1)} %bitcast.90, bf16[2048,2,1024]{0,2,1:T(8,128)(2,1)} %copy-done.1), kind=kOutput, calls=%fused_computation.30 | convolution fusion | flops 1074266112 | bytes 9961472 | tf_op jit(solution)/shard_map/ihj,ihe->jhe/dot_general | solution.py:71
  259.9 0.0 copy-start.7
  259.9 56.9 %reduce-scatter.10.cloned.1.call-done = bf16[128,256]{1,0:T(8,128)(2,1)} async-done(((bf16[2048,256]{1,0:T(8,128)(2,1)}), bf16[128,256]{1,0:T(8,128)(2,1)}) %reduce-scatter.10.cloned.1.call-update) | async-done | bytes 65552
  316.8 2.5 convolution_convert_fusion.1
  319.3 0.0 reduce-scatter.6.cloned.1.call-update
  319.4 0.0 reduce-scatter.8.cloned.1.call-start
  319.4 1.3 fusion.34
  320.7 3.3 add_convert_fusion
  324.1 0.0 reduce-scatter.8.cloned.1.call-update
  324.1 1.5 constant_dynamic-slice_fusion
  325.6 24.3 %reduce-scatter.6.cloned.1.call-done = bf16[128,256]{1,0:T(8,128)(2,1)} async-done(((bf16[128,2048]{1,0:T(8,128)(2,1)}), bf16[128,256]{1,0:T(8,128)(2,1)}) %reduce-scatter.6.cloned.1.call-update) | async-done | bytes 65552 | tf_op jit(solution)/shard_map/reduce_scatter | solution.py:79
  349.9 39.8 %reduce-scatter.8.cloned.1.call-done = bf16[1024,256]{1,0:T(8,128)(2,1)} async-done(((bf16[1024,2048]{1,0:T(8,128)(2,1)}), bf16[1024,256]{1,0:T(8,128)(2,1)}) %reduce-scatter.8.cloned.1.call-update) | async-done | bytes 524304 | tf_op jit(solution)/shard_map/reduce_scatter | solution.py:86
  (16 shorter events, 0.0 us)
Async XLA Ops:
  7.2 4.8 %copy-start = (bf16[2048,256]{1,0:T(8,128)(2,1)S(1)}, bf16[2048,256]{1,0:T(8,128)(2,1)}, u32[]{:S(2)}) copy-start(bf16[2048,256]{1,0:T(8,128)(2,1)} %param.11) | copy-start | bytes 3145732
  7.2 202.4 %all-reduce.2.cloned.1.call-start = ((), (), s32[]{:S(2)}) async-start(), calls=%async_computation.3 | async-start | bytes 4194304 | tf_op jit(solution)/shard_map/psum | solution.py:44
  7.2 4.8 %copy-start.16 = (bf16[1024,2048]{1,0:T(8,128)(2,1)S(1)}, bf16[1024,2048]{1,0:T(8,128)(2,1)}, u32[]{:S(2)}) copy-start(bf16[1024,2048]{1,0:T(8,128)(2,1)} %param.8) | copy-start | bytes 12582916
  7.3 7.6 %slice-start = ((s8[8388608]{0:T(1024)(128)(4,1)}), s8[4194304]{0:T(1024)(128)(4,1)S(1)}, s32[]{:S(2)}) async-start(s8[8388608]{0:T(1024)(128)(4,1)} %bitcast.94), calls=%async_computation.7 | async-start | bytes 8388608
  12.0 1.3 copy-start.15
  12.0 2.8 copy-start.10
  12.0 2.9 slice-start.1
  13.3 3.9 copy-start.5
  14.9 2.4 copy-start.3
  17.3 7.8 %copy-start.8 = (bf16[2048,256]{0,1:T(8,128)(2,1)}, bf16[2048,256]{0,1:T(8,128)(2,1)S(1)}, u32[]{:S(2)}) copy-start(bf16[2048,256]{0,1:T(8,128)(2,1)S(1)} %convolution_convert_fusion) | copy-start | bytes 3145732
  25.0 76.0 %copy-start.11 = (f32[2048,2]{0,1:T(2,128)}, f32[2048,2]{0,1:T(2,128)S(1)}, u32[]{:S(2)}) copy-start(f32[2048,2]{0,1:T(2,128)S(1)} %get-tuple-element.7) | copy-start | bytes 49156
  101.0 8.4 %copy-start.12 = (f32[2048,2]{0,1:T(2,128)S(1)}, f32[2048,2]{0,1:T(2,128)}, u32[]{:S(2)}) copy-start(f32[2048,2]{0,1:T(2,128)} %copy-done.11) | copy-start | bytes 49156
  101.0 8.4 %copy-start.13 = (f32[2048,2]{0,1:T(2,128)S(1)}, f32[2048,2]{0,1:T(2,128)}, u32[]{:S(2)}) copy-start(f32[2048,2]{0,1:T(2,128)} %pmax.7) | copy-start | bytes 49156
  101.0 11.4 %copy-start.2 = (f32[2,1024,2048]{2,1,0:T(8,128)S(1)}, f32[2,1024,2048]{2,1,0:T(8,128)}, u32[]{:S(2)}) copy-start(f32[2,1024,2048]{2,1,0:T(8,128)} %get-tuple-element.8) | copy-start | bytes 50331652
  119.7 75.7 %copy-start.14 = (f32[2048,2]{0,1:T(2,128)S(1)}, f32[2048,2]{0,1:T(2,128)}, u32[]{:S(2)}) copy-start(f32[2048,2]{0,1:T(2,128)} %pmax.7) | copy-start | bytes 49156
  122.7 194.1 %reduce-scatter.10.cloned.1.call-start = ((), (), s32[]{:S(2)}) async-start(), calls=%async_computation.6 | async-start | bytes 1114112
  214.2 14.7 %copy-start.4 = (pred[2048,1024]{0,1:T(8,128)(4,1)S(1)}, pred[2048,1024]{0,1:T(8,128)(4,1)}, u32[]{:S(2)}) copy-start(pred[2048,1024]{0,1:T(8,128)(4,1)} %copy-done.3) | copy-start | bytes 6291460
  228.9 12.8 %copy-start.6 = (bf16[1024,256]{0,1:T(8,128)(2,1)S(1)}, bf16[1024,256]{0,1:T(8,128)(2,1)}, u32[]{:S(2)}) copy-start(bf16[1024,256]{0,1:T(8,128)(2,1)} %copy-done.5) | copy-start | bytes 1572868
  238.5 3.2 copy-start.1
  244.3 9.3 %copy-start.9 = (bf16[2048,256]{0,1:T(8,128)(2,1)S(1)}, bf16[2048,256]{0,1:T(8,128)(2,1)}, u32[]{:S(2)}) copy-start(bf16[2048,256]{0,1:T(8,128)(2,1)} %copy-done.8) | copy-start | bytes 3145732
  244.3 105.6 %reduce-scatter.6.cloned.1.call-start = ((), (), s32[]{:S(2)}) async-start(), calls=%async_computation.4 | async-start | bytes 589824 | tf_op jit(solution)/shard_map/reduce_scatter | solution.py:79
  259.9 60.9 %copy-start.7 = (bf16[2048,256]{1,0:T(8,128)(2,1)S(1)}, bf16[2048,256]{1,0:T(8,128)(2,1)}, u32[]{:S(2)}) copy-start(bf16[2048,256]{1,0:T(8,128)(2,1)} %param.12) | copy-start | bytes 3145732
  319.4 70.3 %reduce-scatter.8.cloned.1.call-start = ((), (), s32[]{:S(2)}) async-start(), calls=%async_computation.5 | async-start | bytes 4718592 | tf_op jit(solution)/shard_map/reduce_scatter | solution.py:86
Sparse Core Ops, SparseCore 0:
  122.8 86.7 all-reduce.1
  244.5 72.2 reduce-scatter.9
  319.7 30.1 reduce-scatter.5
  352.9 36.7 reduce-scatter.7
where the time goes:
time: 397 us; the launch traced here: 396 us
  blocking collectives  146 us (37%)
  waiting for transfers between devices  135 us (34%)
  matrix products  56.7 us (14%)
  local copies, waits for them, and re-layouts  23.5 us (6%)
  other arithmetic  20.4 us (5%)
  between operations  14.1 us (4%)
    pmax x1, blocking collectives, body(): highest = lax.pmax(local_max, 'seq')  76 us
    psum x1, blocking collectives, body(): totals, merged = lax.psum((local_sum * factor, scaled_out), 'seq')  70 us
    unnamed x5, waiting for transfers between devices  57 us
    reduce_scatter x1, waiting for transfers between devices, body(): lax.psum_scatter(context_term.astype(jnp.bfloat16), 'head', scatter_dimen...  39.8 us
    reduce_scatter x1, waiting for transfers between devices, body(): lax.psum_scatter(latent_term.astype(jnp.bfloat16), 'head', scatter_dimens...  24.3 us
    psum x1, waiting for transfers between devices, body(): totals, merged = lax.psum((local_sum * factor, scaled_out), 'seq')  14.2 us
    dot_general x1, matrix products, body(): jnp.einsum('ihe,jhe->ihj', grad_heads, value_heads, preferred_element_typ...  9.58 us
    dot_general x1, matrix products, body(): jnp.einsum('ihj,ihe->jhe', probabilities.astype(jnp.bfloat16), grad_heads...  8.97 us
  transfers between devices with their start and end apart: 4, of which 4 were waited for; matrix products, arithmetic and copies ran while one was open for 6% of the time, Pallas kernels for 0%

commit v1 on v0

v1 whole, which is shorter than its diff:
```python
import functools
import math

import jax
import jax.numpy as jnp
from jax import lax
from jax.experimental import pallas as pl
from jax.experimental.pallas import tpu as pltpu
from jax.sharding import PartitionSpec as P

E = 128
SCALE = E ** (-0.5)
TO_LOG2 = SCALE * math.log2(math.e)
FLOOR = -1e30
N_SEQ = 16
N_X = 4
LAT = 2048
TOK = 1024
COLS = 256
WIDE = 2048
PAIR = 256
N_PAIR = LAT // PAIR
CHUNK = 256
N_CHUNK = TOK // CHUNK
MESH = pl.DeviceIdType.MESH
BF = jnp.bfloat16
F32 = jnp.float32

NT = (((1,), (1,)), ((), ()))


def dot(a, b):
    return jnp.dot(a, b, preferred_element_type=F32)


def dot_nt(a, b):
    return lax.dot_general(a, b, NT, preferred_element_type=F32)


def kernel(
    lat_hbm, ctx_hbm, off_ref, wq_hbm, wk_hbm, wv_hbm, go_hbm,
    att_ref, gl_ref, gc_ref,
    lat, ctx, wq, wk, wv, go,
    goT, k_s, v_s, kT, vT, qT, wT,
    sflat, sbuf, srecv, obuf, orecv, res, resrecv, rows,
    gosT, fqT, dqT, dqbuf, dqrecv, dkv,
    ctxb, sibrecv, sums, arecv, bsend, brecv,
    ltb, lsib, lsums, larecv, lbsend, lbrecv,
    in_sem, st_s, st_r, o_s, o_r, rs_s, rs_r, dq_s, dq_r, sib_s, sib_r, a_s, a_r, b_s, b_r,
):
    seq = lax.axis_index("seq")
    head = lax.axis_index("head")
    core = lax.rem(head, 2)
    x = head // 2
    x_right, x_left = lax.rem(x + 1, N_X), lax.rem(x + 3, N_X)
    x_far = lax.rem(x + 2, N_X)
    sibling = x * 2 + 1 - core
    right, left = x_right * 2 + core, x_left * 2 + core

    def peer(k):
        return lax.rem(seq + k, N_SEQ)

    def load(src, dst, n):
        return pltpu.make_async_copy(src, dst, in_sem.at[n])

    def load_pair(t):
        p = lax.rem(seq // 2 + t, N_PAIR)
        return pltpu.make_async_copy(lat_hbm.at[pl.ds(p * PAIR, PAIR)], lat.at[t], in_sem.at[8 + t])

    load(wk_hbm, wk, 0).start()
    for c in range(N_CHUNK):
        rows_c = pl.ds(c * CHUNK, CHUNK)
        load(ctx_hbm.at[rows_c], ctx.at[rows_c], 4 + c).start()
        if c == 0:
            load(wv_hbm, wv, 1).start()
    load(go_hbm, go, 3).start()
    load(wq_hbm, wq, 2).start()
    for t in range(N_PAIR):
        load_pair(t).start()

    barrier = pltpu.get_barrier_semaphore()
    for k in range(1, N_SEQ):
        pl.semaphore_signal(barrier, inc=1, device_id=(peer(k), head), device_id_type=MESH)
    for h in (sibling, right, left):
        pl.semaphore_signal(barrier, inc=1, device_id=(seq, h), device_id_type=MESH)
    pl.semaphore_wait(barrier, N_SEQ - 1 + 3)

    load(wk_hbm, wk, 0).wait()
    for c in range(N_CHUNK):
        rows_c = pl.ds(c * CHUNK, CHUNK)
        load(ctx_hbm.at[rows_c], ctx.at[rows_c], 4 + c).wait()
        if c == 0:
            load(wv_hbm, wv, 1).wait()
        block = ctx[rows_c, :]
        kb = dot(block, wk[...]).astype(BF)
        k_s[rows_c, :] = kb
        kT[:, rows_c] = kb.T
        vb = dot(block, wv[...]).astype(BF)
        v_s[rows_c, :] = vb
        vT[:, rows_c] = vb.T
    load(go_hbm, go, 3).wait()

    def turn(p, _):
        at = pl.ds(pl.multiple_of(p * PAIR, PAIR), PAIR)
        goT[:, at] = go[at, :].T
        return 0

    lax.fori_loop(0, N_PAIR, turn, 0)
    load(wq_hbm, wq, 2).wait()

    def stat_copy(h, b, k):
        return pltpu.make_async_remote_copy(
            src_ref=sbuf.at[h, b], dst_ref=srecv.at[h, k], send_sem=st_s.at[h, k], recv_sem=st_r.at[h, k],
            device_id=(b, head), device_id_type=MESH)

    def out_copy(h, b, k):
        return pltpu.make_async_remote_copy(
            src_ref=obuf.at[h, b], dst_ref=orecv.at[h, k], send_sem=o_s.at[h, k], recv_sem=o_r.at[h, k],
            device_id=(b, head), device_id_type=MESH)

    def res_copy(h, k):
        return pltpu.make_async_remote_copy(
            src_ref=res.at[h], dst_ref=resrecv.at[h, seq], send_sem=rs_s.at[h, k], recv_sem=rs_r.at[h, k],
            device_id=(peer(k), head), device_id_type=MESH)

    def res_wait(h, k):
        other = lax.rem(seq + N_SEQ - k, N_SEQ)
        return pltpu.make_async_remote_copy(
            src_ref=res.at[h], dst_ref=resrecv.at[h, other], send_sem=rs_s.at[h, k], recv_sem=rs_r.at[h, k],
            device_id=(peer(k), head), device_id_type=MESH)

    def dq_copy(h, k):
        return pltpu.make_async_remote_copy(
            src_ref=dqbuf.at[h, peer(k)], dst_ref=dqrecv.at[h, k], send_sem=dq_s.at[h, k], recv_sem=dq_r.at[h, k],
            device_id=(peer(k), head), device_id_type=MESH)

    def forward(h, t):
        p = lax.rem(seq // 2 + t, N_PAIR)
        at = pl.ds(pl.multiple_of(p * PAIR, PAIR), PAIR)
        hs = slice(h * E, (h + 1) * E)
        if h == 0:
            pltpu.make_async_copy(lat_hbm.at[pl.ds(p * PAIR, PAIR)], lat.at[t], in_sem.at[8 + t]).wait()
            qT[:, at] = dot(lat[t], wq[...]).astype(BF).T
        s = dot(k_s[:, hs], qT[hs, at]) * TO_LOG2
        bound = off_ref[p] - seq * TOK
        s = jnp.where(lax.broadcasted_iota(jnp.int32, (TOK, PAIR), 0) <= bound, s, FLOOR)
        m = jnp.max(s, axis=0, keepdims=True)
        w = jnp.exp2(s - m)
        total = jnp.sum(w, axis=0, keepdims=True)
        wb = w.astype(BF)
        wT[h, :, at] = wb
        o = dot(vT[hs, :], wb)
        d = jnp.sum(goT[hs, at].astype(F32) * o, axis=0, keepdims=True)
        st = jnp.concatenate([m, total, d, jnp.zeros((5, PAIR), F32)], axis=0)
        sflat[h, :, at] = st
        ob = o.astype(BF)
        for half in range(2):
            b = 2 * p + half
            part = slice(half * 128, (half + 1) * 128)
            sbuf[h, b] = st[:, part]
            obuf[h, b] = ob[:, part]
            k = lax.rem(b - seq + N_SEQ, N_SEQ)

            @pl.when(b != seq)
            def _():
                stat_copy(h, b, k).start()
                out_copy(h, b, k).start()

    def combine(h):
        for k in range(1, N_SEQ):
            stat_copy(h, peer(k), k).wait_recv()
        own = sbuf[h, seq]
        everyone = [own] + [srecv[h, k] for k in range(1, N_SEQ)]
        top = functools.reduce(jnp.maximum, [e[0:1] for e in everyone])
        factors = [jnp.exp2(e[0:1] - top) for e in everyone]
        total = sum(e[1:2] * f for e, f in zip(everyone, factors))
        d = sum(e[2:3] * f for e, f in zip(everyone, factors)) / total
        lse = top + jnp.log2(total)
        both = jnp.concatenate([lse, d, jnp.zeros((6, 128), F32)], axis=0)
        res[h] = both
        resrecv[h, seq] = both
        for k in range(1, N_SEQ):
            res_copy(h, k).start()
        for k in range(N_SEQ):
            rows[h, k] = jnp.broadcast_to(factors[k] / total, (8, 128))

    def answers(h):
        hs = slice(h * E, (h + 1) * E)
        for k in range(1, N_SEQ):
            res_wait(h, k).wait_recv()
        lse = jnp.concatenate([resrecv[h, b, 0:1, :] for b in range(N_SEQ)], axis=1)
        delta = jnp.concatenate([resrecv[h, b, 1:2, :] for b in range(N_SEQ)], axis=1)
        f = jnp.exp2(sflat[h, 0:1, :] - lse)
        gosT[...] = (goT[hs, :].astype(F32) * f).astype(BF)
        fqT[...] = (qT[hs, :].astype(F32) * f).astype(BF)
        sflat[h, 3:4, :] = delta
        sflat[h, 4:5, :] = f * SCALE

    def backward(h, c):
        hs = slice(h * E, (h + 1) * E)
        rc = pl.ds(pl.multiple_of(c * CHUNK, CHUNK), CHUNK)
        w = wT[h, rc, :]
        dp = dot(v_s[rc, hs], goT[hs, :])
        ds = (w.astype(F32) * (dp - sflat[h, 3:4, :])).astype(BF)
        dkv[rc, h * E : (h + 1) * E] = (dot_nt(ds, fqT[...]) * SCALE).astype(BF)
        dkv[rc, COLS + h * E : COLS + (h + 1) * E] = dot_nt(w, gosT[...]).astype(BF)
        dqT[...] += dot(kT[hs, rc], ds)

    def send_query(h):
        for b in range(N_SEQ):
            at = slice(b * 128, (b + 1) * 128)
            dqbuf[h, b] = (dqT[:, at] * sflat[h, 4:5, at]).astype(BF)
        for k in range(1, N_SEQ):
            dq_copy(h, k).start()

    class Reduce:
        def __init__(self, n, term, sib, total, a_in, b_out, b_in, half):
            self.n, self.term, self.sib, self.total = n, term, sib, total
            self.a_in, self.b_out, self.b_in, self.half = a_in, b_out, b_in, half

        def to(self, src, dst, ss, rs, h):
            return pltpu.make_async_remote_copy(
                src_ref=src, dst_ref=dst, send_sem=ss, recv_sem=rs, device_id=(seq, h), device_id_type=MESH)

        def c_sib(self):
            return self.to(self.term.at[1 - core], self.sib, sib_s.at[self.n], sib_r.at[self.n], sibling)

        def c_a(self, way):
            part = pl.ds(way * self.half, self.half)
            return self.to(self.total.at[x_far, part], self.a_in.at[way], a_s.at[self.n, way], a_r.at[self.n, way],
                           (right, left)[way])

        def c_b(self, way):
            return self.to(self.b_out.at[way], self.b_in.at[way], b_s.at[self.n, way], b_r.at[self.n, way],
                           (right, left)[way])

        def step_sib(self):
            self.c_sib().start()

        def step_a(self):
            self.c_sib().wait_recv()
            for j in range(N_X):
                self.total[j] = (self.term[core, j].astype(F32) + self.sib[j].astype(F32)).astype(BF)
            for way in range(2):
                self.c_a(way).start()

        def step_b(self):
            for way in range(2):
                self.c_a(way).wait_recv()
                to = (x_right, x_left)[way]
                mine, other = pl.ds(way * self.half, self.half), pl.ds((1 - way) * self.half, self.half)
                self.b_out[way, mine, :] = (
                    self.total[to, mine, :].astype(F32) + self.a_in[way].astype(F32)).astype(BF)
                self.b_out[way, other, :] = self.total[to, other, :]
                self.c_b(way).start()

        def finish(self):
            for way in range(2):
                self.c_b(way).wait_recv()
            return (self.total[x].astype(F32) + self.b_in[0].astype(F32) + self.b_in[1].astype(F32)).astype(BF)

        def drain(self):
            self.c_sib().wait_send()
            for way in range(2):
                self.c_a(way).wait_send()
                self.c_b(way).wait_send()

    parts = [
        Reduce(c, ctxb.at[c], sibrecv.at[c], sums.at[c], arecv.at[c], bsend.at[c], brecv.at[c], CHUNK // 2)
        for c in range(N_CHUNK)
    ]
    latent_part = Reduce(N_CHUNK, ltb, lsib, lsums, larecv, lbsend, lbrecv, 64)

    def loop(n, f):
        def step(i, _):
            f(i)
            return 0

        lax.fori_loop(0, n, step, 0)

    loop(N_PAIR, lambda t: forward(0, t))
    loop(N_PAIR // 2, lambda t: forward(1, t))
    combine(0)
    loop(N_PAIR // 2, lambda t: forward(1, t + N_PAIR // 2))
    answers(0)
    dqT[...] = jnp.zeros_like(dqT)
    loop(N_CHUNK // 2, lambda c: backward(0, c))
    combine(1)
    loop(N_CHUNK // 2, lambda c: backward(0, c + N_CHUNK // 2))
    send_query(0)
    answers(1)
    dqT[...] = jnp.zeros_like(dqT)

    def context_term(c):
        rc = pl.ds(c * CHUNK, CHUNK)
        for n in range(8):
            at = slice(n * COLS, (n + 1) * COLS)
            term = dot_nt(dkv[rc, 0:COLS], wk[at, :]) + dot_nt(dkv[rc, COLS:], wv[at, :])
            ctxb[c, n % 2, n // 2] = term.astype(BF)

    for c in range(N_CHUNK):
        backward(1, c)
        if c == N_CHUNK - 1:
            send_query(1)
        context_term(c)
        parts[c].step_sib()
        if c >= 1:
            parts[c - 1].step_a()
        if c >= 2:
            parts[c - 2].step_b()
    parts[N_CHUNK - 1].step_a()
    parts[N_CHUNK - 2].step_b()

    for h in range(2):
        for k in range(1, N_SEQ):
            dq_copy(h, k).wait_recv()
    dq = jnp.concatenate(
        [
            dqbuf[h, seq].astype(F32) + sum(dqrecv[h, k].astype(F32) for k in range(1, N_SEQ))
            for h in range(2)
        ],
        axis=0,
    ).astype(BF).T
    for n in range(8):
        ltb[n % 2, n // 2] = dot_nt(dq, wq[n * COLS : (n + 1) * COLS, :]).astype(BF)
    latent_part.step_sib()
    parts[N_CHUNK - 1].step_b()
    latent_part.step_a()

    for h in range(2):
        for k in range(1, N_SEQ):
            out_copy(h, peer(k), k).wait_recv()
        o = obuf[h, seq].astype(F32) * rows[h, 0, 0:1, :]
        for k in range(1, N_SEQ):
            o = o + orecv[h, k].astype(F32) * rows[h, k, 0:1, :]
        att_ref[:, h * E : (h + 1) * E] = o.T.astype(BF)
    latent_part.step_b()
    for c in range(N_CHUNK):
        gc_ref[c * CHUNK : (c + 1) * CHUNK, :] = parts[c].finish()
    gl_ref[...] = latent_part.finish()

    for h in range(2):
        for k in range(1, N_SEQ):
            stat_copy(h, peer(k), k).wait_send()
            out_copy(h, peer(k), k).wait_send()
            res_copy(h, k).wait_send()
            dq_copy(h, k).wait_send()
    for part in [*parts, latent_part]:
        part.drain()


def body(latents, context, offsets, w_query, w_key, w_value, grad_out):
    hbm = pl.BlockSpec(memory_space=pl.ANY)
    vmem = pl.BlockSpec(memory_space=pltpu.VMEM)
    v, dma = pltpu.VMEM, pltpu.SemaphoreType.DMA
    return pl.pallas_call(
        kernel,
        out_shape=(
            jax.ShapeDtypeStruct((LAT // N_SEQ, COLS), BF),
            jax.ShapeDtypeStruct((LAT // N_SEQ, COLS), BF),
            jax.ShapeDtypeStruct((TOK, COLS), BF),
        ),
        in_specs=[hbm, hbm, vmem, hbm, hbm, hbm, hbm],
        out_specs=(vmem, vmem, vmem),
        scratch_shapes=[
            v((N_PAIR, PAIR, WIDE), BF),
            v((TOK, WIDE), BF),
            v((WIDE, COLS), BF),
            v((WIDE, COLS), BF),
            v((WIDE, COLS), BF),
            v((LAT, COLS), BF),
            v((COLS, LAT), BF),
            v((TOK, COLS), BF),
            v((TOK, COLS), BF),
            v((COLS, TOK), BF),
            v((COLS, TOK), BF),
            v((COLS, LAT), BF),
            v((2, TOK, LAT), BF),
            v((2, 8, LAT), F32),
            v((2, N_SEQ, 8, 128), F32),
            v((2, N_SEQ, 8, 128), F32),
            v((2, N_SEQ, 128, 128), BF),
            v((2, N_SEQ, 128, 128), BF),
            v((2, 8, 128), F32),
            v((2, N_SEQ, 8, 128), F32),
            v((2, N_SEQ, 8, 128), F32),
            v((E, LAT), BF),
            v((E, LAT), BF),
            v((E, LAT), F32),
            v((2, N_SEQ, 128, 128), BF),
            v((2, N_SEQ, 128, 128), BF),
            v((TOK, 2 * COLS), BF),
            v((N_CHUNK, 2, N_X, CHUNK, COLS), BF),
            v((N_CHUNK, N_X, CHUNK, COLS), BF),
            v((N_CHUNK, N_X, CHUNK, COLS), BF),
            v((N_CHUNK, 2, CHUNK // 2, COLS), BF),
            v((N_CHUNK, 2, CHUNK, COLS), BF),
            v((N_CHUNK, 2, CHUNK, COLS), BF),
            v((2, N_X, 128, COLS), BF),
            v((N_X, 128, COLS), BF),
            v((N_X, 128, COLS), BF),
            v((2, 64, COLS), BF),
            v((2, 128, COLS), BF),
            v((2, 128, COLS), BF),
            dma((16,)),
            *[dma((2, N_SEQ))] * 8,
            dma((N_CHUNK + 1,)),
            dma((N_CHUNK + 1,)),
            *[dma((N_CHUNK + 1, 2))] * 4,
        ],
        compiler_params=pltpu.CompilerParams(
            collective_id=0, has_side_effects=True, vmem_limit_bytes=60 * 1024 * 1024
        ),
        cost_estimate=pl.CostEstimate(flops=13_000_000_000, bytes_accessed=20_000_000, transcendentals=4_200_000),
    )(latents, context, offsets.reshape(N_PAIR, 1, PAIR), w_query, w_key, w_value, grad_out)


def solution(mesh):
    placed = (
        P(),
        P("seq", None),
        P(),
        P(None, "head"),
        P(None, "head"),
        P(None, "head"),
        P(None, "head"),
    )
    return jax.shard_map(
        body,
        mesh=mesh,
        in_specs=placed,
        out_specs=(P("seq", "head"), P("seq", "head"), P("seq", "head")),
        check_vma=False,
    )
```

time: 397 us -> 81.9 us (0.21)
  blocking collectives: 146 us -> 0 us
  waiting for transfers between devices: 135 us -> 0 us
  Pallas kernels: 0 us -> 76.2 us
  matrix products: 56.7 us -> 0 us
  other arithmetic: 20.4 us -> 0 us
  local copies, waits for them, and re-layouts: 23.5 us -> 4.81 us
  between operations: 14.1 us -> 0.64 us
    pallas_call x0 -> x1, Pallas kernels: none -> 76.2 us  [body(): pl.pallas_call(kernel, out_shape=(jax.ShapeDtypeStruct((LAT // N_SEQ, COL...]
    pmax x1 -> x0, blocking collectives: 76 us -> none  [body(): highest = lax.pmax(local_max, 'seq')]
    psum x1 -> x0, blocking collectives: 70 us -> none  [body(): totals, merged = lax.psum((local_sum * factor, scaled_out), 'seq')]
    reduce_scatter x2 -> x0, waiting for transfers between devices: 64.1 us -> none  [the longest x1 39.8 us: body(): lax.psum_scatter(context_term.astype(jnp.bfloat16), 'head', scatter_dimen...]
    unnamed x5 -> x0, waiting for transfers between devices: 57 us -> none
    dot_general x12 -> x0, matrix products: 56.7 us -> none  [the longest x1 9.58 us: body(): jnp.einsum('ihe,jhe->ihj', grad_heads, value_heads, preferred_element_typ...]
    psum x1 -> x0, waiting for transfers between devices: 14.2 us -> none  [body(): totals, merged = lax.psum((local_sum * factor, scaled_out), 'seq')]
    reduce_sum x2 -> x0, other arithmetic: 14 us -> none  [the longest x1 8.41 us: body(): local_sum = jnp.sum(weights, axis=2)]
  transfers between devices with their start and end apart: 4 -> 0, of which waited for: 4 -> 0; matrix products, arithmetic and copies ran while one was open for 6% -> 0% of each run, Pallas kernels for 0% -> 0%
where the time goes in v1:
time: 81.9 us; the launch traced here: 81.6 us
  Pallas kernels  76.2 us (93%)
  local copies, waits for them, and re-layouts  4.81 us (6%)
    pallas_call x1, Pallas kernels, body(): pl.pallas_call(kernel, out_shape=(jax.ShapeDtypeStruct((LAT // N_SEQ, COL...  76.2 us
    unnamed x3, local copies, waits for them, and re-layouts  4.81 us

profile of v1, /device:TPU:0, one launch (start us, length us, event | category | flops | bytes accessed | tf_op | source)
XLA Modules:
  0.0 81.6 jit_solution(5099086695131203313)
XLA Ops:
  0.6 76.2 %shard_map.94 = (bf16[128,256]{1,0:T(8,128)(2,1)}, bf16[128,256]{1,0:T(8,128)(2,1)}, bf16[1024,256]{1,0:T(8,128)(2,1)}) custom-call(bf16[2048,2048]{1,0:T(8,128)(2,1)} %lat_hbm.1, bf16[1024,2048]{1,0:T(8,128)(2,1)} %ctx_hbm.1, s32[8,1,256]{2,1,0:T(1,128)} %bitcast.1, bf16[2048,256]{1,0:T(8,128)(2,1)} %wq_hbm.1, bf16[2048,256]{1,0:T(8,128)(2,1)} %wk_hbm.1, ...), custom_call_target="tpu_custom_call" | custom-call | flops 12999999488 | bytes 20000000 | tf_op jit(solution)/shard_map/pallas_call | solution.py:356
  76.8 1.5 %copy.13 = bf16[128,256]{1,0:T(8,128)(2,1)} copy(bf16[128,256]{1,0:T(8,128)(2,1)} %get-tuple-element.6) | data formatting | bytes 131072
  78.3 1.5 %copy.14 = bf16[128,256]{1,0:T(8,128)(2,1)} copy(bf16[128,256]{1,0:T(8,128)(2,1)} %get-tuple-element.7) | data formatting | bytes 131072
  79.7 1.9 %copy.15 = bf16[1024,256]{1,0:T(8,128)(2,1)} copy(bf16[1024,256]{1,0:T(8,128)(2,1)} %get-tuple-element.8) | data formatting | bytes 1048576

commit v2 on v0

v2 whole, which is shorter than its diff:
```python
import functools
import math

import jax
import jax.numpy as jnp
from jax import lax
from jax.experimental import pallas as pl
from jax.experimental.pallas import tpu as pltpu
from jax.sharding import PartitionSpec as P

E = 128
SCALE = E ** (-0.5)
TO_LOG2 = SCALE * math.log2(math.e)
FLOOR = -1e30
N_SEQ = 16
LAT = 2048
TOK = 1024
COLS = 256
WIDE = 2048
PAIR = 256
N_PAIR = LAT // PAIR
CHUNK = 256
N_CHUNK = TOK // CHUNK
RINGS = 2
MESH = pl.DeviceIdType.MESH
BF = jnp.bfloat16
F32 = jnp.float32

NT = (((1,), (1,)), ((), ()))


def dot(a, b):
    return jnp.dot(a, b, preferred_element_type=F32)


def dot_nt(a, b):
    return lax.dot_general(a, b, NT, preferred_element_type=F32)


class Ring:
    def __init__(self, n, sems, where, ends, total, a_in, b_out, b_in, half):
        self.n, self.sems, self.half = n, sems, half
        self.me, self.right, self.left, self.far = where
        self.ends = ends
        self.total, self.a_in, self.b_out, self.b_in = total, a_in, b_out, b_in

    def copy(self, src, dst, s, r, way):
        return pltpu.make_async_remote_copy(
            src_ref=src, dst_ref=dst, send_sem=s.at[self.n, way], recv_sem=r.at[self.n, way],
            device_id=self.ends[way], device_id_type=MESH)

    def c_a(self, way):
        part = pl.ds(way * self.half, self.half)
        return self.copy(self.total.at[self.far, part], self.a_in.at[way], self.sems[0], self.sems[1], way)

    def c_b(self, way):
        return self.copy(self.b_out.at[way], self.b_in.at[way], self.sems[2], self.sems[3], way)

    def step_a(self):
        for way in range(2):
            self.c_a(way).start()

    def step_b(self):
        for way in range(2):
            self.c_a(way).wait_recv()
            to = (self.right, self.left)[way]
            mine, other = pl.ds(way * self.half, self.half), pl.ds((1 - way) * self.half, self.half)
            self.b_out[way, mine, :] = (self.total[to, mine, :].astype(F32) + self.a_in[way].astype(F32)).astype(BF)
            self.b_out[way, other, :] = self.total[to, other, :]
            self.c_b(way).start()

    def finish(self):
        for way in range(2):
            self.c_b(way).wait_recv()
        return self.total[self.me].astype(F32) + self.b_in[0].astype(F32) + self.b_in[1].astype(F32)

    def drain(self):
        for way in range(2):
            self.c_a(way).wait_send()
            self.c_b(way).wait_send()


def kernel(
    lat_hbm, ctx_hbm, off_hbm, wq_hbm, wk_hbm, wv_hbm, go_hbm,
    att_out, gl_out, gc_out,
    att_ref, gl_ref, gc_ref,
    off_ref, lat, wq, wkv, go,
    goT, k_s, v_s, kT, v1T, qT, wT, sc, mrow,
    mflat, fflat, sbuf, srecv, obuf,
    gosT, fqT, dqT, dkv, tot1, r1, tot2, r2,
    ctxb, sibrecv, arecv, bsend, brecv, xrecv,
    ltb, lsib, lrecv,
    in_sem, st_s, st_r, f_s, f_r, sib_s, sib_r, a_s, a_r, b_s, b_r, x_s, x_r, out_sem,
):
    seq = lax.axis_index("seq")
    head = lax.axis_index("head")
    core, x = lax.rem(head, 2), head // 2
    y, z = lax.rem(seq, 4), seq // 4
    ring_sems = (a_s, a_r, b_s, b_r)
    on_x, on_y, on_z = ([lax.rem(at + i, 4) for i in (0, 1, 3, 2)] for at in (x, y, z))
    x_ends = [(seq, i * 2 + core) for i in on_x[1:]]
    y_ends = [(z * 4 + i, head) for i in on_y[1:]]
    z_ends = [(i * 4 + y, head) for i in on_z[1:]]
    sibling = (seq, x * 2 + 1 - core)

    def peer(k):
        return lax.rem(seq + k, N_SEQ)

    def remote(src, dst, ss, rs, to):
        return pltpu.make_async_remote_copy(
            src_ref=src, dst_ref=dst, send_sem=ss, recv_sem=rs, device_id=to, device_id_type=MESH)

    def load(src, dst, n):
        return pltpu.make_async_copy(src, dst, in_sem.at[n])

    def load_context(c):
        rc = pl.ds(c * CHUNK, CHUNK)
        return load(ctx_hbm.at[rc], wT.at[0, rc], 4 + c)

    def load_pair(p):
        return load(lat_hbm.at[pl.ds(p * PAIR, PAIR)], lat.at[p], 8 + p)

    load_k = load(wk_hbm, wkv.at[:, pl.ds(0, COLS)], 0)
    load_v = load(wv_hbm, wkv.at[:, pl.ds(COLS, COLS)], 1)
    load_q = load(wq_hbm, wq, 2)
    load_g = load(go_hbm, go, 3)
    load_offsets = load(off_hbm, off_ref, 16)
    load_k.start()
    load_v.start()
    for c in range(N_CHUNK):
        load_context(c).start()

    barrier = pltpu.get_barrier_semaphore()
    for k in range(1, N_SEQ):
        pl.semaphore_signal(barrier, inc=1, device_id=(peer(k), head), device_id_type=MESH)
    for end in [sibling, *x_ends]:
        pl.semaphore_signal(barrier, inc=1, device_id=end, device_id_type=MESH)

    v1T[:, E:, :] = jnp.ones((2, 16, TOK), BF)
    load_k.wait()
    load_v.wait()
    for c in range(N_CHUNK):
        rc = pl.ds(c * CHUNK, CHUNK)
        load_context(c).wait()
        if c == 0:
            load_q.start()
            load_g.start()
            load_offsets.start()
            load_pair(0).start()
            load_pair(1).start()
        else:
            load_pair(2 * c).start()
            load_pair(2 * c + 1).start()
        both = dot(wT[0, rc, :], wkv[...]).astype(BF)
        kb, vb = both[:, :COLS], both[:, COLS:]
        k_s[rc, :] = kb
        kT[:, rc] = kb.T
        v_s[rc, :] = vb
        vt = vb.T
        for h in range(2):
            v1T[h, 0:E, rc] = vt[h * E : (h + 1) * E, :]
    load_g.wait()

    def lanes(p):
        return pl.ds(pl.multiple_of(p * PAIR, PAIR), PAIR)

    def turn(p, _):
        goT[:, lanes(p)] = go[lanes(p), :].T
        return 0

    lax.fori_loop(0, N_PAIR, turn, 0)
    load_q.wait()
    load_offsets.wait()

    def query(p, acc, n):
        kc = slice(n * 512, (n + 1) * 512)
        return acc + dot(lat[p, :, kc], wq[kc, :])

    def scores(p, h, j, top):
        at = lanes(p)
        hs = slice(h * E, (h + 1) * E)
        s = dot(k_s[j : j + CHUNK, hs], qT[hs, at])
        bound = off_ref[p] - (seq * TOK + j)
        s = jnp.where(lax.broadcasted_iota(jnp.int32, (CHUNK, PAIR), 0) <= bound, s, FLOOR)
        sc[h, j : j + CHUNK, :] = s
        m = jnp.max(s, axis=0, keepdims=True)
        return m if top is None else jnp.maximum(top, m)

    def stat_copy(p, k):
        return remote(sbuf.at[p], srecv.at[p, k], st_s.at[0], st_r.at[p], (peer(k), head))

    def wait_bytes(ref, sem):
        pltpu.make_async_copy(ref, ref, sem).wait()

    def forward(p, ahead, further):
        at = lanes(p)
        top = [mrow[h, 0:1, :] * TO_LOG2 for h in range(2)]
        out, then, acc = [0.0, 0.0], [None, None], 0.0
        if further:
            load_pair(p + 2).wait()
        for n in range(N_CHUNK):
            j = n * CHUNK
            for h in range(2):
                w = jnp.exp2(sc[h, j : j + CHUNK, :] * TO_LOG2 - top[h]).astype(BF)
                wT[h, j : j + CHUNK, at] = w
                out[h] = out[h] + dot(v1T[h, :, j : j + CHUNK], w)
                if ahead:
                    then[h] = scores(p + 1, h, j, then[h])
            if further:
                acc = query(p + 2, acc, n)
        if further:
            qT[:, lanes(p + 2)] = acc.astype(BF).T
        lse, delta = [], []
        for h in range(2):
            hs = slice(h * E, (h + 1) * E)
            total = out[h][E : E + 1]
            o = out[h][:E] / total
            d = jnp.sum(goT[hs, at].astype(F32) * o, axis=0, keepdims=True)
            mflat[h, :, at] = jnp.broadcast_to(top[h], (8, PAIR))
            if ahead:
                mrow[h] = jnp.broadcast_to(then[h], (8, PAIR))
            both = top[h] + jnp.log2(total)
            lse += [both[:, :128], both[:, 128:]]
            delta += [d[:, :128], d[:, 128:]]
            ob = o.astype(BF)
            for half in range(2):
                obuf[2 * p + half, hs, :] = ob[:, half * 128 : (half + 1) * 128]
        sbuf[p] = jnp.concatenate(lse + delta, axis=0)
        for k in range(1, N_SEQ):
            stat_copy(p, k).start()

    def merge(p):
        wait_bytes(srecv.at[p, pl.ds(1, N_SEQ - 1)], st_r.at[p])
        everyone = [sbuf[p]] + [srecv[p, k] for k in range(1, N_SEQ)]
        top = functools.reduce(jnp.maximum, [e[0:4] for e in everyone])
        factors = [jnp.exp2(e[0:4] - top) for e in everyone]
        total = sum(factors)
        delta = sum(e[4:8] * f for e, f in zip(everyone, factors)) / total
        lse = top + jnp.log2(total)
        share = factors[0] / total
        at = slice(p * PAIR, (p + 1) * PAIR)
        for h in range(2):
            hs = slice(h * E, (h + 1) * E)
            rows = [jnp.concatenate([a[2 * h : 2 * h + 1], a[2 * h + 1 : 2 * h + 2]], axis=1) for a in (lse, delta, share)]
            f = jnp.exp2(mflat[h, 0:1, at] - rows[0])
            fflat[h, 0:1, at] = f
            fflat[h, 1:2, at] = rows[1]
            fflat[h, 2:3, at] = rows[2]
            gosT[hs, at] = (goT[hs, at].astype(F32) * f).astype(BF)
            fqT[hs, at] = (qT[hs, at].astype(F32) * f).astype(BF)

    def grad_scores(h, c):
        hs = slice(h * E, (h + 1) * E)
        rc = pl.ds(c * CHUNK, CHUNK)
        dp = dot(v_s[rc, hs], goT[hs, :])
        ds = (wT[h, rc, :].astype(F32) * (dp - fflat[h, 1:2, :])).astype(BF)
        lat[h * N_CHUNK + c] = ds
        dq = dot(kT[hs, rc], ds)
        dqT[hs, :] = dq if c == 0 else dqT[hs, :] + dq

    class Blocks:
        def __init__(self, i):
            self.i = i
            self.axes = ((on_y, y_ends), (on_z, z_ends))

        def copies(self, h, stage):
            on, ends = self.axes[h ^ stage]
            src, dst = ((tot1, r1), (tot2, r2))[stage]
            n = 4 * self.i + 2 * h + stage
            return [
                remote(src.at[self.i, h, on[d + 1]], dst.at[self.i, h, d], f_s.at[n], f_r.at[n], ends[d]) for d in range(3)
            ]

        def start(self, h, block):
            for b in range(N_SEQ):
                to, row = (b % 4, b // 4) if h == 0 else (b // 4, b % 4)
                tot1[self.i, h, to, row * 128 : (row + 1) * 128, :] = block(h, b).astype(BF)
            for copy in self.copies(h, 0):
                copy.start()

        def total(self, h, stage):
            src, dst = ((tot1, r1), (tot2, r2))[stage]
            wait_bytes(dst.at[self.i, h], f_r.at[4 * self.i + 2 * h + stage])
            me = self.axes[h ^ stage][0][0]
            return src[self.i, h, me].astype(F32) + sum(dst[self.i, h, d].astype(F32) for d in range(3))

        def second(self, h):
            got = self.total(h, 0).astype(BF)
            for j in range(4):
                tot2[self.i, h, j] = got[j * 128 : (j + 1) * 128, :]
            for copy in self.copies(h, 1):
                copy.start()

        def finish(self, h):
            return self.total(h, 1)

        def drain(self):
            for h in range(2):
                wait_bytes(r1.at[self.i, h], f_s.at[4 * self.i + 2 * h])
                wait_bytes(r2.at[self.i, h], f_s.at[4 * self.i + 2 * h + 1])

    outs, queries = Blocks(0), Blocks(1)

    def out_block(h, b):
        at = slice(b * 128, (b + 1) * 128)
        return obuf[b, h * E : (h + 1) * E, :].astype(F32) * fflat[h, 2:3, at]

    def query_block(h, b):
        at = slice(b * 128, (b + 1) * 128)
        return dqT[h * E : (h + 1) * E, at] * (fflat[h, 0:1, at] * SCALE)

    def grad_keys_values(h, c):
        rc = pl.ds(c * CHUNK, CHUNK)
        hs = slice(h * E, (h + 1) * E)
        dkv[rc, hs] = (dot_nt(lat[h * N_CHUNK + c], fqT[hs, :]) * SCALE).astype(BF)
        dkv[rc, COLS + h * E : COLS + (h + 1) * E] = dot_nt(wT[h, rc, :], gosT[hs, :]).astype(BF)

    def context_term(c):
        rc = pl.ds(c * CHUNK, CHUNK)
        for n in range(8):
            ctxb[c, n % 2, n // 2] = dot_nt(dkv[rc, :], wkv[n * COLS : (n + 1) * COLS, :]).astype(BF)
        parts[c].sib_start()

    class Heads:
        def __init__(self, n, term, sib, ring, direct):
            self.n, self.sib, self.total = n, sib, term.at[core]
            self.c_sib = remote(term.at[1 - core], sib, sib_s.at[n], sib_r.at[n], sibling)
            self.ring = Ring(n, ring_sems, on_x, x_ends, self.total, *ring) if ring else None
            self.direct = direct

        def copies(self):
            m = self.n - RINGS
            return [remote(self.total.at[on_x[d + 1]], self.direct.at[d], x_s.at[m], x_r.at[m], x_ends[d]) for d in range(3)]

        def sib_start(self):
            self.c_sib.start()

        def a(self):
            self.c_sib.wait_recv()
            for j in range(4):
                self.total[j] = (self.total[j].astype(F32) + self.sib[j].astype(F32)).astype(BF)
            if self.ring:
                self.ring.step_a()
            else:
                for copy in self.copies():
                    copy.start()

        def b(self):
            self.ring.step_b()

        def finish(self):
            if self.ring:
                return self.ring.finish()
            wait_bytes(self.direct, x_r.at[self.n - RINGS])
            return self.total[x].astype(F32) + sum(self.direct[d].astype(F32) for d in range(3))

        def drain(self):
            self.c_sib.wait_send()
            if self.ring:
                self.ring.drain()
            else:
                wait_bytes(self.direct, x_s.at[self.n - RINGS])

    parts = [
        Heads(
            c, ctxb.at[c], sibrecv.at[c],
            (arecv.at[c], bsend.at[c], brecv.at[c], CHUNK // 2) if c < RINGS else None,
            xrecv.at[c - RINGS] if c >= RINGS else None,
        )
        for c in range(N_CHUNK)
    ]
    latent_part = Heads(N_CHUNK, ltb, lsib, None, lrecv)

    for p in range(2):
        load_pair(p).wait()
        qT[:, p * PAIR : (p + 1) * PAIR] = dot(lat[p], wq[...]).astype(BF).T
    for h in range(2):
        m = None
        for j in range(0, TOK, CHUNK):
            m = scores(0, h, j, m)
        mrow[h] = jnp.broadcast_to(m, (8, PAIR))
    pl.semaphore_wait(barrier, N_SEQ - 1 + 4)

    def step(p, _):
        forward(p, True, True)
        return 0

    lax.fori_loop(0, N_PAIR - 2, step, 0)
    forward(N_PAIR - 2, True, False)
    forward(N_PAIR - 1, False, False)
    for p in range(N_PAIR):
        merge(p)
    for h in range(2):
        outs.start(h, out_block)

    grad_scores(0, 0)
    grad_scores(1, 0)
    grad_keys_values(0, 0)
    grad_keys_values(1, 0)
    context_term(0)
    grad_scores(0, 1)
    grad_scores(1, 1)
    grad_keys_values(0, 1)
    parts[0].a()
    grad_keys_values(1, 1)
    context_term(1)
    grad_scores(0, 2)
    grad_scores(0, 3)
    queries.start(0, query_block)
    parts[1].a()
    grad_scores(1, 2)
    grad_scores(1, 3)
    queries.start(1, query_block)
    parts[0].b()
    grad_keys_values(0, 2)
    grad_keys_values(1, 2)
    context_term(2)
    for h in range(2):
        outs.second(h)
    grad_keys_values(0, 3)
    parts[1].b()
    parts[2].a()
    grad_keys_values(1, 3)
    context_term(3)
    queries.second(0)
    parts[3].a()
    queries.second(1)

    def store_context(c):
        rc = pl.ds(c * CHUNK, CHUNK)
        return pltpu.make_async_copy(gc_ref.at[rc], gc_out.at[rc], out_sem.at[c])

    def finish_context(c):
        gc_ref[c * CHUNK : (c + 1) * CHUNK, :] = parts[c].finish().astype(BF)
        store_context(c).start()

    store_attention = pltpu.make_async_copy(att_ref, att_out, out_sem.at[N_CHUNK])
    store_latents = pltpu.make_async_copy(gl_ref, gl_out, out_sem.at[N_CHUNK + 1])

    for h in range(2):
        att_ref[:, h * E : (h + 1) * E] = outs.finish(h).T.astype(BF)
    store_attention.start()

    dq = jnp.concatenate([queries.finish(h) for h in range(2)], axis=0).astype(BF).T
    for n in range(8):
        ltb[n % 2, n // 2] = dot_nt(dq, wq[n * COLS : (n + 1) * COLS, :]).astype(BF)
    latent_part.sib_start()
    finish_context(0)
    latent_part.a()
    for c in range(1, N_CHUNK):
        finish_context(c)
    gl_ref[...] = latent_part.finish().astype(BF)
    store_latents.start()

    wait_bytes(srecv.at[:, pl.ds(1, N_SEQ - 1)], st_s.at[0])
    for part in [*parts, latent_part, outs, queries]:
        part.drain()
    for c in range(N_CHUNK):
        store_context(c).wait()
    store_attention.wait()
    store_latents.wait()


def body(latents, context, offsets, w_query, w_key, w_value, grad_out):
    hbm = pl.BlockSpec(memory_space=pltpu.HBM)
    v, dma = pltpu.VMEM, pltpu.SemaphoreType.DMA
    return pl.pallas_call(
        kernel,
        out_shape=(
            jax.ShapeDtypeStruct((LAT // N_SEQ, COLS), BF),
            jax.ShapeDtypeStruct((LAT // N_SEQ, COLS), BF),
            jax.ShapeDtypeStruct((TOK, COLS), BF),
        ),
        in_specs=[hbm] * 7,
        out_specs=(pl.BlockSpec(memory_space=pl.ANY),) * 3,
        scratch_shapes=[
            v((LAT // N_SEQ, COLS), BF),
            v((LAT // N_SEQ, COLS), BF),
            v((TOK, COLS), BF),
            v((N_PAIR, 1, PAIR), jnp.int32),
            v((N_PAIR, PAIR, WIDE), BF),
            v((WIDE, COLS), BF),
            v((WIDE, 2 * COLS), BF),
            v((LAT, COLS), BF),
            v((COLS, LAT), BF),
            v((TOK, COLS), BF),
            v((TOK, COLS), BF),
            v((COLS, TOK), BF),
            v((2, E + 16, TOK), BF),
            v((COLS, LAT), BF),
            v((2, TOK, LAT), BF),
            v((2, TOK, PAIR), F32),
            v((2, 8, PAIR), F32),
            v((2, 8, LAT), F32),
            v((2, 8, LAT), F32),
            v((N_PAIR, 8, 128), F32),
            v((N_PAIR, N_SEQ, 8, 128), F32),
            v((N_SEQ, COLS, 128), BF),
            v((COLS, LAT), BF),
            v((COLS, LAT), BF),
            v((COLS, LAT), F32),
            v((TOK, 2 * COLS), BF),
            v((2, 2, 4, 512, 128), BF),
            v((2, 2, 3, 512, 128), BF),
            v((2, 2, 4, 128, 128), BF),
            v((2, 2, 3, 128, 128), BF),
            v((N_CHUNK, 2, 4, CHUNK, COLS), BF),
            v((N_CHUNK, 4, CHUNK, COLS), BF),
            v((RINGS, 2, CHUNK // 2, COLS), BF),
            v((RINGS, 2, CHUNK, COLS), BF),
            v((RINGS, 2, CHUNK, COLS), BF),
            v((N_CHUNK - RINGS, 3, CHUNK, COLS), BF),
            v((2, 4, 128, COLS), BF),
            v((4, 128, COLS), BF),
            v((3, 128, COLS), BF),
            dma((17,)),
            dma((1,)),
            dma((N_PAIR,)),
            *[dma((8,))] * 2,
            *[dma((N_CHUNK + 1,))] * 2,
            *[dma((RINGS, 2))] * 4,
            *[dma((N_CHUNK + 1 - RINGS,))] * 2,
            dma((N_CHUNK + 2,)),
        ],
        compiler_params=pltpu.CompilerParams(
            collective_id=0, has_side_effects=True, vmem_limit_bytes=50 * 1024 * 1024
        ),
        cost_estimate=pl.CostEstimate(flops=13_000_000_000, bytes_accessed=20_000_000, transcendentals=4_200_000),
    )(
        *[
            pltpu.with_memory_space_constraint(a, pltpu.HBM)
            for a in (latents, context, offsets.reshape(N_PAIR, 1, PAIR), w_query, w_key, w_value, grad_out)
        ]
    )


def solution(mesh):
    placed = (
        P(),
        P("seq", None),
        P(),
        P(None, "head"),
        P(None, "head"),
        P(None, "head"),
        P(None, "head"),
    )
    return jax.shard_map(
        body,
        mesh=mesh,
        in_specs=placed,
        out_specs=(P("seq", "head"), P("seq", "head"), P("seq", "head")),
        check_vma=False,
    )
```

time: 397 us -> 61.2 us (0.15)
  blocking collectives: 146 us -> 0 us
  waiting for transfers between devices: 135 us -> 0 us
  Pallas kernels: 0 us -> 57.7 us
  matrix products: 56.7 us -> 0 us
  local copies, waits for them, and re-layouts: 23.5 us -> 2.05 us
  other arithmetic: 20.4 us -> 0 us
  between operations: 14.1 us -> 0.64 us
    pmax x1 -> x0, blocking collectives: 76 us -> none  [body(): highest = lax.pmax(local_max, 'seq')]
    psum x1 -> x0, blocking collectives: 70 us -> none  [body(): totals, merged = lax.psum((local_sum * factor, scaled_out), 'seq')]
    reduce_scatter x2 -> x0, waiting for transfers between devices: 64.1 us -> none  [the longest x1 39.8 us: body(): lax.psum_scatter(context_term.astype(jnp.bfloat16), 'head', scatter_dimen...]
    pallas_call x0 -> x1, Pallas kernels: none -> 57.7 us  [body(): pl.pallas_call(kernel, out_shape=(jax.ShapeDtypeStruct((LAT // N_SEQ, COL...]
    unnamed x5 -> x0, waiting for transfers between devices: 57 us -> none
    dot_general x12 -> x0, matrix products: 56.7 us -> none  [the longest x1 9.58 us: body(): jnp.einsum('ihe,jhe->ihj', grad_heads, value_heads, preferred_element_typ...]
    psum x1 -> x0, waiting for transfers between devices: 14.2 us -> none  [body(): totals, merged = lax.psum((local_sum * factor, scaled_out), 'seq')]
    reduce_sum x2 -> x0, other arithmetic: 14 us -> none  [the longest x1 8.41 us: body(): local_sum = jnp.sum(weights, axis=2)]
  transfers between devices with their start and end apart: 4 -> 0, of which waited for: 4 -> 0; matrix products, arithmetic and copies ran while one was open for 6% -> 0% of each run, Pallas kernels for 0% -> 0%
where the time goes in v2:
time: 61.2 us; the launch traced here: 60.4 us
  Pallas kernels  57.7 us (94%)
  local copies, waits for them, and re-layouts  2.05 us (3%)
  between operations  0.64 us (1%)
    pallas_call x1, Pallas kernels, body(): pl.pallas_call(kernel, out_shape=(jax.ShapeDtypeStruct((LAT // N_SEQ, COL...  57.7 us
    unnamed x3, local copies, waits for them, and re-layouts  2.05 us

profile of v2, /device:TPU:0, one launch (start us, length us, event | category | flops | bytes accessed | tf_op | source)
XLA Modules:
  0.0 60.4 jit_solution(13726059365796376683)
XLA Ops:
  0.6 57.7 %shard_map.94 = (bf16[128,256]{1,0:T(8,128)(2,1)S(1)}, bf16[128,256]{1,0:T(8,128)(2,1)S(1)}, bf16[1024,256]{1,0:T(8,128)(2,1)S(1)}) custom-call(bf16[2048,2048]{1,0:T(8,128)(2,1)} %lat_hbm.1, bf16[1024,2048]{1,0:T(8,128)(2,1)} %ctx_hbm.1, s32[8,1,256]{2,1,0:T(1,128)} %bitcast.1, bf16[2048,256]{1,0:T(8,128)(2,1)} %wq_hbm.1, bf16[2048,256]{1,0:T(8,128)(2,1)} %wk_hbm.1, ...), custom_call_target="tpu_custom_call" | custom-call | flops 12999999488 | bytes 20000000 | tf_op jit(solution)/shard_map/pallas_call | solution.py:467
  58.3 0.6 %copy.13 = bf16[128,256]{1,0:T(8,128)(2,1)} copy(bf16[128,256]{1,0:T(8,128)(2,1)S(1)} %get-tuple-element.6) | data formatting | bytes 131072
  58.9 0.6 %copy.14 = bf16[128,256]{1,0:T(8,128)(2,1)} copy(bf16[128,256]{1,0:T(8,128)(2,1)S(1)} %get-tuple-element.7) | data formatting | bytes 131072
  59.6 0.8 %copy.15 = bf16[1024,256]{1,0:T(8,128)(2,1)} copy(bf16[1024,256]{1,0:T(8,128)(2,1)S(1)} %get-tuple-element.8) | data formatting | bytes 1048576

commit v3 on v2

--- a/solution.py
+++ b/solution.py
@@ -21,7 +21,8 @@
 N_PAIR = LAT // PAIR
 CHUNK = 256
 N_CHUNK = TOK // CHUNK
-RINGS = 2
+CHUNKS = ((0, 128), (128, 128), (256, 256), (512, 256), (768, 256))
+N_PART = len(CHUNKS)
 MESH = pl.DeviceIdType.MESH
 BF = jnp.bfloat16
 F32 = jnp.float32
@@ -87,10 +88,10 @@
     off_ref, lat, wq, wkv, go,
     goT, k_s, v_s, kT, v1T, qT, wT, sc, mrow,
     mflat, fflat, sbuf, srecv, obuf,
-    gosT, fqT, dqT, dkv, tot1, r1, tot2, r2,
-    ctxb, sibrecv, arecv, bsend, brecv, xrecv,
+    gosT, fqT, dqT, dkv, tot1, r1, tot2, r2, dqbuf, dqrecv,
+    ctxb, sibrecv, arecv, bsend, brecv,
     ltb, lsib, lrecv,
-    in_sem, st_s, st_r, f_s, f_r, sib_s, sib_r, a_s, a_r, b_s, b_r, x_s, x_r, out_sem,
+    in_sem, st_s, st_r, f_s, f_r, dq_s, dq_r, sib_s, sib_r, a_s, a_r, b_s, b_r, x_s, x_r, out_sem,
 ):
     seq = lax.axis_index("seq")
     head = lax.axis_index("head")
@@ -123,12 +124,22 @@
     load_k = load(wk_hbm, wkv.at[:, pl.ds(0, COLS)], 0)
     load_v = load(wv_hbm, wkv.at[:, pl.ds(COLS, COLS)], 1)
     load_q = load(wq_hbm, wq, 2)
-    load_g = load(go_hbm, go, 3)
+    def load_grad(p):
+        rows = pl.ds(p * PAIR, PAIR)
+        return load(go_hbm.at[rows], go.at[rows], 17 + p)
+
     load_offsets = load(off_hbm, off_ref, 16)
+    load_q.start()
+    load_pair(0).start()
+    load_pair(1).start()
     load_k.start()
     load_v.start()
-    for c in range(N_CHUNK):
-        load_context(c).start()
+    load_context(0).start()
+    load_context(1).start()
+    for p in range(N_PAIR):
+        load_grad(p).start()
+    load_context(2).start()
+    load_context(3).start()
 
     barrier = pltpu.get_barrier_semaphore()
     for k in range(1, N_SEQ):
@@ -137,39 +148,40 @@
         pl.semaphore_signal(barrier, inc=1, device_id=end, device_id_type=MESH)
 
     v1T[:, E:, :] = jnp.ones((2, 16, TOK), BF)
+    def lanes(p):
+        return pl.ds(pl.multiple_of(p * PAIR, PAIR), PAIR)
+
+    def turn(c):
+        rc = pl.ds(c * CHUNK, CHUNK)
+        kT[:, rc] = k_s[rc, :].T
+        vt = v_s[rc, :].T
+        for h in range(2):
+            v1T[h, 0:E, rc] = vt[h * E : (h + 1) * E, :]
+
+    load_q.wait()
+    for p in range(2):
+        load_pair(p).wait()
+        qT[:, p * PAIR : (p + 1) * PAIR] = dot(lat[p], wq[...]).astype(BF).T
     load_k.wait()
     load_v.wait()
     for c in range(N_CHUNK):
         rc = pl.ds(c * CHUNK, CHUNK)
         load_context(c).wait()
         if c == 0:
-            load_q.start()
-            load_g.start()
             load_offsets.start()
-            load_pair(0).start()
-            load_pair(1).start()
         else:
             load_pair(2 * c).start()
             load_pair(2 * c + 1).start()
+        pieces = range(3 * (c - 1), min(3 * c, N_PAIR)) if c else ()
+        for p in pieces:
+            load_grad(p).wait()
         both = dot(wT[0, rc, :], wkv[...]).astype(BF)
-        kb, vb = both[:, :COLS], both[:, COLS:]
-        k_s[rc, :] = kb
-        kT[:, rc] = kb.T
-        v_s[rc, :] = vb
-        vt = vb.T
-        for h in range(2):
-            v1T[h, 0:E, rc] = vt[h * E : (h + 1) * E, :]
-    load_g.wait()
-
-    def lanes(p):
-        return pl.ds(pl.multiple_of(p * PAIR, PAIR), PAIR)
-
-    def turn(p, _):
-        goT[:, lanes(p)] = go[lanes(p), :].T
-        return 0
-
-    lax.fori_loop(0, N_PAIR, turn, 0)
-    load_q.wait()
+        if c:
+            turn(c - 1)
+        for p in pieces:
+            goT[:, p * PAIR : (p + 1) * PAIR] = go[p * PAIR : (p + 1) * PAIR, :].T
+        k_s[rc, :] = both[:, :COLS]
+        v_s[rc, :] = both[:, COLS:]
     load_offsets.wait()
 
     def query(p, acc, n):
@@ -249,45 +261,51 @@
             gosT[hs, at] = (goT[hs, at].astype(F32) * f).astype(BF)
             fqT[hs, at] = (qT[hs, at].astype(F32) * f).astype(BF)
 
+    def rows_of(c):
+        return pl.ds(*CHUNKS[c])
+
+    def kept(h, c):
+        start, size = CHUNKS[c]
+        return lat.at[h * N_CHUNK + start // CHUNK, pl.ds(start % CHUNK, size)]
+
     def grad_scores(h, c):
         hs = slice(h * E, (h + 1) * E)
-        rc = pl.ds(c * CHUNK, CHUNK)
-        dp = dot(v_s[rc, hs], goT[hs, :])
+        rc = rows_of(c)
+        if c == 0:
+            dp = jnp.concatenate([sc[h, p * 128 : (p + 1) * 128, :] for p in range(N_PAIR)], axis=1)
+        else:
+            dp = dot(v_s[rc, hs], goT[hs, :])
         ds = (wT[h, rc, :].astype(F32) * (dp - fflat[h, 1:2, :])).astype(BF)
-        lat[h * N_CHUNK + c] = ds
+        kept(h, c)[...] = ds
         dq = dot(kT[hs, rc], ds)
         dqT[hs, :] = dq if c == 0 else dqT[hs, :] + dq
 
     class Blocks:
-        def __init__(self, i):
-            self.i = i
-            self.axes = ((on_y, y_ends), (on_z, z_ends))
+        axes = ((on_y, y_ends), (on_z, z_ends))
 
         def copies(self, h, stage):
             on, ends = self.axes[h ^ stage]
             src, dst = ((tot1, r1), (tot2, r2))[stage]
-            n = 4 * self.i + 2 * h + stage
-            return [
-                remote(src.at[self.i, h, on[d + 1]], dst.at[self.i, h, d], f_s.at[n], f_r.at[n], ends[d]) for d in range(3)
-            ]
+            n = 2 * h + stage
+            return [remote(src.at[h, on[d + 1]], dst.at[h, d], f_s.at[n], f_r.at[n], ends[d]) for d in range(3)]
 
         def start(self, h, block):
             for b in range(N_SEQ):
                 to, row = (b % 4, b // 4) if h == 0 else (b // 4, b % 4)
-                tot1[self.i, h, to, row * 128 : (row + 1) * 128, :] = block(h, b).astype(BF)
+                tot1[h, to, row * 128 : (row + 1) * 128, :] = block(h, b).astype(BF)
             for copy in self.copies(h, 0):
                 copy.start()
 
         def total(self, h, stage):
             src, dst = ((tot1, r1), (tot2, r2))[stage]
-            wait_bytes(dst.at[self.i, h], f_r.at[4 * self.i + 2 * h + stage])
+            wait_bytes(dst.at[h], f_r.at[2 * h + stage])
             me = self.axes[h ^ stage][0][0]
-            return src[self.i, h, me].astype(F32) + sum(dst[self.i, h, d].astype(F32) for d in range(3))
+            return src[h, me].astype(F32) + sum(dst[h, d].astype(F32) for d in range(3))
 
         def second(self, h):
             got = self.total(h, 0).astype(BF)
             for j in range(4):
-                tot2[self.i, h, j] = got[j * 128 : (j + 1) * 128, :]
+                tot2[h, j] = got[j * 128 : (j + 1) * 128, :]
             for copy in self.copies(h, 1):
                 copy.start()
 
@@ -296,41 +314,50 @@
 
         def drain(self):
             for h in range(2):
-                wait_bytes(r1.at[self.i, h], f_s.at[4 * self.i + 2 * h])
-                wait_bytes(r2.at[self.i, h], f_s.at[4 * self.i + 2 * h + 1])
-
-    outs, queries = Blocks(0), Blocks(1)
+                wait_bytes(r1.at[h], f_s.at[2 * h])
+                wait_bytes(r2.at[h], f_s.at[2 * h + 1])
+
+    outs = Blocks()
 
     def out_block(h, b):
         at = slice(b * 128, (b + 1) * 128)
         return obuf[b, h * E : (h + 1) * E, :].astype(F32) * fflat[h, 2:3, at]
 
-    def query_block(h, b):
-        at = slice(b * 128, (b + 1) * 128)
-        return dqT[h * E : (h + 1) * E, at] * (fflat[h, 0:1, at] * SCALE)
+    def send_query(h):
+        for b in range(N_SEQ):
+            at = slice(b * 128, (b + 1) * 128)
+            dqbuf[h, b] = (dqT[h * E : (h + 1) * E, at] * (fflat[h, 0:1, at] * SCALE)).astype(BF)
+        for k in range(1, N_SEQ):
+            remote(dqbuf.at[h, peer(k)], dqrecv.at[h, k], dq_s.at[h], dq_r.at[h], (peer(k), head)).start()
+
+    def own_query(h):
+        wait_bytes(dqrecv.at[h, pl.ds(1, N_SEQ - 1)], dq_r.at[h])
+        return dqbuf[h, seq].astype(F32) + sum(dqrecv[h, k].astype(F32) for k in range(1, N_SEQ))
 
     def grad_keys_values(h, c):
-        rc = pl.ds(c * CHUNK, CHUNK)
+        rc = rows_of(c)
         hs = slice(h * E, (h + 1) * E)
-        dkv[rc, hs] = (dot_nt(lat[h * N_CHUNK + c], fqT[hs, :]) * SCALE).astype(BF)
+        dkv[rc, hs] = (dot_nt(kept(h, c)[...], fqT[hs, :]) * SCALE).astype(BF)
         dkv[rc, COLS + h * E : COLS + (h + 1) * E] = dot_nt(wT[h, rc, :], gosT[hs, :]).astype(BF)
 
+    def term_of(c):
+        start, size = CHUNKS[c]
+        return ctxb.at[start // CHUNK, :, :, pl.ds(start % CHUNK, size)]
+
     def context_term(c):
-        rc = pl.ds(c * CHUNK, CHUNK)
+        rc = rows_of(c)
         for n in range(8):
-            ctxb[c, n % 2, n // 2] = dot_nt(dkv[rc, :], wkv[n * COLS : (n + 1) * COLS, :]).astype(BF)
+            term_of(c)[n % 2, n // 2] = dot_nt(dkv[rc, :], wkv[n * COLS : (n + 1) * COLS, :]).astype(BF)
         parts[c].sib_start()
 
     class Heads:
-        def __init__(self, n, term, sib, ring, direct):
+        def __init__(self, n, term, sib, ring):
             self.n, self.sib, self.total = n, sib, term.at[core]
             self.c_sib = remote(term.at[1 - core], sib, sib_s.at[n], sib_r.at[n], sibling)
             self.ring = Ring(n, ring_sems, on_x, x_ends, self.total, *ring) if ring else None
-            self.direct = direct
 
         def copies(self):
-            m = self.n - RINGS
-            return [remote(self.total.at[on_x[d + 1]], self.direct.at[d], x_s.at[m], x_r.at[m], x_ends[d]) for d in range(3)]
+            return [remote(self.total.at[on_x[d + 1]], lrecv.at[d], x_s.at[0], x_r.at[0], x_ends[d]) for d in range(3)]
 
         def sib_start(self):
             self.c_sib.start()
@@ -351,29 +378,26 @@
         def finish(self):
             if self.ring:
                 return self.ring.finish()
-            wait_bytes(self.direct, x_r.at[self.n - RINGS])
-            return self.total[x].astype(F32) + sum(self.direct[d].astype(F32) for d in range(3))
+            wait_bytes(lrecv, x_r.at[0])
+            return self.total[x].astype(F32) + sum(lrecv[d].astype(F32) for d in range(3))
 
         def drain(self):
             self.c_sib.wait_send()
             if self.ring:
                 self.ring.drain()
             else:
-                wait_bytes(self.direct, x_s.at[self.n - RINGS])
-
-    parts = [
-        Heads(
-            c, ctxb.at[c], sibrecv.at[c],
-            (arecv.at[c], bsend.at[c], brecv.at[c], CHUNK // 2) if c < RINGS else None,
-            xrecv.at[c - RINGS] if c >= RINGS else None,
-        )
-        for c in range(N_CHUNK)
-    ]
-    latent_part = Heads(N_CHUNK, ltb, lsib, None, lrecv)
-
-    for p in range(2):
-        load_pair(p).wait()
-        qT[:, p * PAIR : (p + 1) * PAIR] = dot(lat[p], wq[...]).astype(BF).T
+                wait_bytes(lrecv, x_s.at[0])
+
+    def part(c):
+        start, size = CHUNKS[c]
+        block, rc = start // CHUNK, pl.ds(start % CHUNK, size)
+        ring = (arecv.at[block, :, pl.ds(start % CHUNK // 2, size // 2)], bsend.at[block, :, rc], brecv.at[block, :, rc])
+        return Heads(c, term_of(c), sibrecv.at[block, :, rc], (*ring, size // 2))
+
+    parts = [part(c) for c in range(N_PART)]
+    latent_part = Heads(N_PART, ltb, lsib, None)
+
+    turn(N_CHUNK - 1)
     for h in range(2):
         m = None
         for j in range(0, TOK, CHUNK):
@@ -388,74 +412,88 @@
     lax.fori_loop(0, N_PAIR - 2, step, 0)
     forward(N_PAIR - 2, True, False)
     forward(N_PAIR - 1, False, False)
-    for p in range(N_PAIR):
+    for p in range(N_PAIR - 1):
         merge(p)
     for h in range(2):
+        hs = slice(h * E, (h + 1) * E)
+        for p in range(N_PAIR):
+            sc[h, p * 128 : (p + 1) * 128, :] = dot(v_s[0:128, hs], goT[hs, p * PAIR : (p + 1) * PAIR])
+    merge(N_PAIR - 1)
+    for h in range(2):
         outs.start(h, out_block)
 
-    grad_scores(0, 0)
-    grad_scores(1, 0)
-    grad_keys_values(0, 0)
-    grad_keys_values(1, 0)
+    def both_heads(f, c):
+        for h in range(2):
+            f(h, c)
+
+    both_heads(grad_scores, 0)
+    both_heads(grad_keys_values, 0)
     context_term(0)
-    grad_scores(0, 1)
-    grad_scores(1, 1)
-    grad_keys_values(0, 1)
+    both_heads(grad_scores, 1)
+    both_heads(grad_keys_values, 1)
     parts[0].a()
-    grad_keys_values(1, 1)
     context_term(1)
-    grad_scores(0, 2)
-    grad_scores(0, 3)
-    queries.start(0, query_block)
+    for c in (2, 3, 4):
+        grad_scores(0, c)
+    send_query(0)
     parts[1].a()
     grad_scores(1, 2)
-    grad_scores(1, 3)
-    queries.start(1, query_block)
+    grad_keys_values(0, 2)
     parts[0].b()
-    grad_keys_values(0, 2)
     grad_keys_values(1, 2)
     context_term(2)
+    grad_scores(1, 3)
+    grad_scores(1, 4)
+    send_query(1)
+    parts[2].a()
+    parts[1].b()
+    both_heads(grad_keys_values, 3)
+    context_term(3)
+    grad_keys_values(0, 4)
+    parts[2].b()
+    grad_keys_values(1, 4)
+    parts[3].a()
+    context_term(4)
     for h in range(2):
         outs.second(h)
-    grad_keys_values(0, 3)
-    parts[1].b()
-    parts[2].a()
-    grad_keys_values(1, 3)
-    context_term(3)
-    queries.second(0)
-    parts[3].a()
-    queries.second(1)
+    parts[4].a()
+    parts[3].b()
 
     def store_context(c):
-        rc = pl.ds(c * CHUNK, CHUNK)
+        rc = rows_of(c)
         return pltpu.make_async_copy(gc_ref.at[rc], gc_out.at[rc], out_sem.at[c])
 
     def finish_context(c):
-        gc_ref[c * CHUNK : (c + 1) * CHUNK, :] = parts[c].finish().astype(BF)
+        gc_ref[rows_of(c), :] = parts[c].finish().astype(BF)
         store_context(c).start()
 
-    store_attention = pltpu.make_async_copy(att_ref, att_out, out_sem.at[N_CHUNK])
-    store_latents = pltpu.make_async_copy(gl_ref, gl_out, out_sem.at[N_CHUNK + 1])
+    store_attention = pltpu.make_async_copy(att_ref, att_out, out_sem.at[N_PART])
+    store_latents = pltpu.make_async_copy(gl_ref, gl_out, out_sem.at[N_PART + 1])
+
+    dq = jnp.concatenate([own_query(h) for h in range(2)], axis=0).astype(BF).T
+    for n in range(8):
+        ltb[n % 2, n // 2] = dot_nt(dq, wq[n * COLS : (n + 1) * COLS, :]).astype(BF)
+    latent_part.sib_start()
+    parts[4].b()
 
     for h in range(2):
         att_ref[:, h * E : (h + 1) * E] = outs.finish(h).T.astype(BF)
     store_attention.start()
-
-    dq = jnp.concatenate([queries.finish(h) for h in range(2)], axis=0).astype(BF).T
-    for n in range(8):
-        ltb[n % 2, n // 2] = dot_nt(dq, wq[n * COLS : (n + 1) * COLS, :]).astype(BF)
-    latent_part.sib_start()
+    latent_part.a()
     finish_context(0)
-    latent_part.a()
-    for c in range(1, N_CHUNK):
-        finish_context(c)
+    finish_context(1)
+    finish_context(2)
+    finish_context(3)
+    finish_context(4)
     gl_ref[...] = latent_part.finish().astype(BF)
     store_latents.start()
 
     wait_bytes(srecv.at[:, pl.ds(1, N_SEQ - 1)], st_s.at[0])
-    for part in [*parts, latent_part, outs, queries]:
+    for h in range(2):
+        wait_bytes(dqrecv.at[h, pl.ds(1, N_SEQ - 1)], dq_s.at[h])
+    for part in [*parts, latent_part, outs]:
         part.drain()
-    for c in range(N_CHUNK):
+    for c in range(N_PART):
         store_context(c).wait()
     store_attention.wait()
     store_latents.wait()
@@ -500,27 +538,29 @@
             v((COLS, LAT), BF),
             v((COLS, LAT), F32),
             v((TOK, 2 * COLS), BF),
-            v((2, 2, 4, 512, 128), BF),
-            v((2, 2, 3, 512, 128), BF),
-            v((2, 2, 4, 128, 128), BF),
-            v((2, 2, 3, 128, 128), BF),
+            v((2, 4, 512, 128), BF),
+            v((2, 3, 512, 128), BF),
+            v((2, 4, 128, 128), BF),
+            v((2, 3, 128, 128), BF),
+            v((2, N_SEQ, 128, 128), BF),
+            v((2, N_SEQ, 128, 128), BF),
             v((N_CHUNK, 2, 4, CHUNK, COLS), BF),
             v((N_CHUNK, 4, CHUNK, COLS), BF),
-            v((RINGS, 2, CHUNK // 2, COLS), BF),
-            v((RINGS, 2, CHUNK, COLS), BF),
-            v((RINGS, 2, CHUNK, COLS), BF),
-            v((N_CHUNK - RINGS, 3, CHUNK, COLS), BF),
+            v((N_CHUNK, 2, CHUNK // 2, COLS), BF),
+            v((N_CHUNK, 2, CHUNK, COLS), BF),
+            v((N_CHUNK, 2, CHUNK, COLS), BF),
             v((2, 4, 128, COLS), BF),
             v((4, 128, COLS), BF),
             v((3, 128, COLS), BF),
-            dma((17,)),
+            dma((25,)),
             dma((1,)),
             dma((N_PAIR,)),
-            *[dma((8,))] * 2,
-            *[dma((N_CHUNK + 1,))] * 2,
-            *[dma((RINGS, 2))] * 4,
-            *[dma((N_CHUNK + 1 - RINGS,))] * 2,
-            dma((N_CHUNK + 2,)),
+            *[dma((4,))] * 2,
+            *[dma((2,))] * 2,
+            *[dma((N_PART + 1,))] * 2,
+            *[dma((N_PART, 2))] * 4,
+            *[dma((1,))] * 2,
+            dma((N_PART + 2,)),
         ],
         compiler_params=pltpu.CompilerParams(
             collective_id=0, has_side_effects=True, vmem_limit_bytes=50 * 1024 * 1024

time: 61.2 us -> 58.4 us (0.954); the launches traced: 60.4 us -> 58.3 us
  Pallas kernels: 57.7 us -> 55.6 us
    pallas_call x1, Pallas kernels: 57.7 us -> 55.6 us  [body(): pl.pallas_call(kernel, out_shape=(jax.ShapeDtypeStruct((LAT // N_SEQ, COL...]
where the time goes in v3:
time: 58.4 us; the launch traced here: 58.3 us
  Pallas kernels  55.6 us (95%)
  local copies, waits for them, and re-layouts  2.05 us (4%)
  between operations  0.64 us (1%)
    pallas_call x1, Pallas kernels, body(): pl.pallas_call(kernel, out_shape=(jax.ShapeDtypeStruct((LAT // N_SEQ, COL...  55.6 us
    unnamed x3, local copies, waits for them, and re-layouts  2.05 us

profile of v3, /device:TPU:0, one launch (start us, length us, event | category | flops | bytes accessed | tf_op | source)
XLA Modules:
  0.0 58.3 jit_solution(5855821481490859025)
XLA Ops:
  0.6 55.6 %shard_map.94 = (bf16[128,256]{1,0:T(8,128)(2,1)S(1)}, bf16[128,256]{1,0:T(8,128)(2,1)S(1)}, bf16[1024,256]{1,0:T(8,128)(2,1)S(1)}) custom-call(bf16[2048,2048]{1,0:T(8,128)(2,1)} %lat_hbm.1, bf16[1024,2048]{1,0:T(8,128)(2,1)} %ctx_hbm.1, s32[8,1,256]{2,1,0:T(1,128)} %bitcast.1, bf16[2048,256]{1,0:T(8,128)(2,1)} %wq_hbm.1, bf16[2048,256]{1,0:T(8,128)(2,1)} %wk_hbm.1, ...), custom_call_target="tpu_custom_call" | custom-call | flops 12999999488 | bytes 20000000 | tf_op jit(solution)/shard_map/pallas_call | solution.py:505
  56.2 0.6 %copy.13 = bf16[128,256]{1,0:T(8,128)(2,1)} copy(bf16[128,256]{1,0:T(8,128)(2,1)S(1)} %get-tuple-element.6) | data formatting | bytes 131072
  56.9 0.6 %copy.14 = bf16[128,256]{1,0:T(8,128)(2,1)} copy(bf16[128,256]{1,0:T(8,128)(2,1)S(1)} %get-tuple-element.7) | data formatting | bytes 131072
  57.5 0.8 %copy.15 = bf16[1024,256]{1,0:T(8,128)(2,1)} copy(bf16[1024,256]{1,0:T(8,128)(2,1)S(1)} %get-tuple-element.8) | data formatting | bytes 1048576

commit v4 on v3

--- a/solution.py
+++ b/solution.py
@@ -47,7 +47,7 @@
 
     def copy(self, src, dst, s, r, way):
         return pltpu.make_async_remote_copy(
-            src_ref=src, dst_ref=dst, send_sem=s.at[self.n, way], recv_sem=r.at[self.n, way],
+            src_ref=src, dst_ref=dst, send_sem=s.at[self.n // N_PART], recv_sem=r.at[self.n, way],
             device_id=self.ends[way], device_id_type=MESH)
 
     def c_a(self, way):
@@ -75,23 +75,18 @@
             self.c_b(way).wait_recv()
         return self.total[self.me].astype(F32) + self.b_in[0].astype(F32) + self.b_in[1].astype(F32)
 
-    def drain(self):
-        for way in range(2):
-            self.c_a(way).wait_send()
-            self.c_b(way).wait_send()
-
 
 def kernel(
     lat_hbm, ctx_hbm, off_hbm, wq_hbm, wk_hbm, wv_hbm, go_hbm,
     att_out, gl_out, gc_out,
     att_ref, gl_ref, gc_ref,
     off_ref, lat, wq, wkv, go,
-    goT, k_s, v_s, kT, v1T, qT, wT, sc, mrow,
+    goT, k_s, v_s, kT, v1T, qT, wT, sc, sc1, mrow,
     mflat, fflat, sbuf, srecv, obuf,
     gosT, fqT, dqT, dkv, tot1, r1, tot2, r2, dqbuf, dqrecv,
     ctxb, sibrecv, arecv, bsend, brecv,
-    ltb, lsib, lrecv,
-    in_sem, st_s, st_r, f_s, f_r, dq_s, dq_r, sib_s, sib_r, a_s, a_r, b_s, b_r, x_s, x_r, out_sem,
+    ltb, lsib, larecv, lbsend, lbrecv,
+    in_sem, st_s, st_r, f_s, f_r, dq_s, dq_r, sib_s, sib_r, a_s, a_r, b_s, b_r, out_sem,
 ):
     seq = lax.axis_index("seq")
     head = lax.axis_index("head")
@@ -124,9 +119,9 @@
     load_k = load(wk_hbm, wkv.at[:, pl.ds(0, COLS)], 0)
     load_v = load(wv_hbm, wkv.at[:, pl.ds(COLS, COLS)], 1)
     load_q = load(wq_hbm, wq, 2)
-    def load_grad(p):
-        rows = pl.ds(p * PAIR, PAIR)
-        return load(go_hbm.at[rows], go.at[rows], 17 + p)
+    def load_grad(g):
+        rows = pl.ds(g * 3 * PAIR, min(3, N_PAIR - 3 * g) * PAIR)
+        return load(go_hbm.at[rows], go.at[rows], 17 + g)
 
     load_offsets = load(off_hbm, off_ref, 16)
     load_q.start()
@@ -136,8 +131,8 @@
     load_v.start()
     load_context(0).start()
     load_context(1).start()
-    for p in range(N_PAIR):
-        load_grad(p).start()
+    for g in range(3):
+        load_grad(g).start()
     load_context(2).start()
     load_context(3).start()
 
@@ -164,24 +159,28 @@
         qT[:, p * PAIR : (p + 1) * PAIR] = dot(lat[p], wq[...]).astype(BF).T
     load_k.wait()
     load_v.wait()
-    for c in range(N_CHUNK):
-        rc = pl.ds(c * CHUNK, CHUNK)
-        load_context(c).wait()
-        if c == 0:
-            load_offsets.start()
-        else:
-            load_pair(2 * c).start()
-            load_pair(2 * c + 1).start()
-        pieces = range(3 * (c - 1), min(3 * c, N_PAIR)) if c else ()
-        for p in pieces:
-            load_grad(p).wait()
-        both = dot(wT[0, rc, :], wkv[...]).astype(BF)
-        if c:
-            turn(c - 1)
+    load_offsets.start()
+    for c in range(2, N_PAIR):
+        load_pair(c).start()
+
+    def turn_grad(pieces):
         for p in pieces:
             goT[:, p * PAIR : (p + 1) * PAIR] = go[p * PAIR : (p + 1) * PAIR, :].T
+
+    for n in range(2):
+        rc = pl.ds(2 * n * CHUNK, 2 * CHUNK)
+        load_context(2 * n).wait()
+        load_context(2 * n + 1).wait()
+        for g in range(3) if n else ():
+            load_grad(g).wait()
+        both = dot(wT[0, rc, :], wkv[...]).astype(BF)
+        if n:
+            turn(0)
+            turn(1)
+            turn_grad(range(N_PAIR))
         k_s[rc, :] = both[:, :COLS]
         v_s[rc, :] = both[:, COLS:]
+    turn(2)
     load_offsets.wait()
 
     def query(p, acc, n):
@@ -271,8 +270,8 @@
     def grad_scores(h, c):
         hs = slice(h * E, (h + 1) * E)
         rc = rows_of(c)
-        if c == 0:
-            dp = jnp.concatenate([sc[h, p * 128 : (p + 1) * 128, :] for p in range(N_PAIR)], axis=1)
+        if c < 2:
+            dp = jnp.concatenate([early[c][h, p * 128 : (p + 1) * 128, :] for p in range(N_PAIR)], axis=1)
         else:
             dp = dot(v_s[rc, hs], goT[hs, :])
         ds = (wT[h, rc, :].astype(F32) * (dp - fflat[h, 1:2, :])).astype(BF)
@@ -353,11 +352,8 @@
     class Heads:
         def __init__(self, n, term, sib, ring):
             self.n, self.sib, self.total = n, sib, term.at[core]
-            self.c_sib = remote(term.at[1 - core], sib, sib_s.at[n], sib_r.at[n], sibling)
-            self.ring = Ring(n, ring_sems, on_x, x_ends, self.total, *ring) if ring else None
-
-        def copies(self):
-            return [remote(self.total.at[on_x[d + 1]], lrecv.at[d], x_s.at[0], x_r.at[0], x_ends[d]) for d in range(3)]
+            self.c_sib = remote(term.at[1 - core], sib, sib_s.at[n // N_PART], sib_r.at[n], sibling)
+            self.ring = Ring(n, ring_sems, on_x, x_ends, self.total, *ring)
 
         def sib_start(self):
             self.c_sib.start()
@@ -366,27 +362,13 @@
             self.c_sib.wait_recv()
             for j in range(4):
                 self.total[j] = (self.total[j].astype(F32) + self.sib[j].astype(F32)).astype(BF)
-            if self.ring:
-                self.ring.step_a()
-            else:
-                for copy in self.copies():
-                    copy.start()
+            self.ring.step_a()
 
         def b(self):
             self.ring.step_b()
 
         def finish(self):
-            if self.ring:
-                return self.ring.finish()
-            wait_bytes(lrecv, x_r.at[0])
-            return self.total[x].astype(F32) + sum(lrecv[d].astype(F32) for d in range(3))
-
-        def drain(self):
-            self.c_sib.wait_send()
-            if self.ring:
-                self.ring.drain()
-            else:
-                wait_bytes(lrecv, x_s.at[0])
+            return self.ring.finish()
 
     def part(c):
         start, size = CHUNKS[c]
@@ -395,7 +377,7 @@
         return Heads(c, term_of(c), sibrecv.at[block, :, rc], (*ring, size // 2))
 
     parts = [part(c) for c in range(N_PART)]
-    latent_part = Heads(N_PART, ltb, lsib, None)
+    latent_part = Heads(N_PART, ltb, lsib, (larecv, lbsend, lbrecv, 64))
 
     turn(N_CHUNK - 1)
     for h in range(2):
@@ -414,10 +396,12 @@
     forward(N_PAIR - 1, False, False)
     for p in range(N_PAIR - 1):
         merge(p)
-    for h in range(2):
-        hs = slice(h * E, (h + 1) * E)
-        for p in range(N_PAIR):
-            sc[h, p * 128 : (p + 1) * 128, :] = dot(v_s[0:128, hs], goT[hs, p * PAIR : (p + 1) * PAIR])
+    early = (sc, sc1)
+    for c in range(2):
+        for h in range(2):
+            hs = slice(h * E, (h + 1) * E)
+            for p in range(N_PAIR):
+                early[c][h, p * 128 : (p + 1) * 128, :] = dot(v_s[rows_of(c), hs], goT[hs, p * PAIR : (p + 1) * PAIR])
     merge(N_PAIR - 1)
     for h in range(2):
         outs.start(h, out_block)
@@ -431,8 +415,8 @@
     context_term(0)
     both_heads(grad_scores, 1)
     both_heads(grad_keys_values, 1)
+    context_term(1)
     parts[0].a()
-    context_term(1)
     for c in (2, 3, 4):
         grad_scores(0, c)
     send_query(0)
@@ -445,15 +429,15 @@
     grad_scores(1, 3)
     grad_scores(1, 4)
     send_query(1)
+    grad_keys_values(0, 3)
+    parts[1].b()
     parts[2].a()
-    parts[1].b()
-    both_heads(grad_keys_values, 3)
+    grad_keys_values(1, 3)
     context_term(3)
-    grad_keys_values(0, 4)
-    parts[2].b()
-    grad_keys_values(1, 4)
+    both_heads(grad_keys_values, 4)
     parts[3].a()
     context_term(4)
+    parts[2].b()
     for h in range(2):
         outs.second(h)
     parts[4].a()
@@ -474,15 +458,16 @@
     for n in range(8):
         ltb[n % 2, n // 2] = dot_nt(dq, wq[n * COLS : (n + 1) * COLS, :]).astype(BF)
     latent_part.sib_start()
-    parts[4].b()
 
     for h in range(2):
         att_ref[:, h * E : (h + 1) * E] = outs.finish(h).T.astype(BF)
     store_attention.start()
     latent_part.a()
+    parts[4].b()
     finish_context(0)
     finish_context(1)
     finish_context(2)
+    latent_part.b()
     finish_context(3)
     finish_context(4)
     gl_ref[...] = latent_part.finish().astype(BF)
@@ -491,8 +476,10 @@
     wait_bytes(srecv.at[:, pl.ds(1, N_SEQ - 1)], st_s.at[0])
     for h in range(2):
         wait_bytes(dqrecv.at[h, pl.ds(1, N_SEQ - 1)], dq_s.at[h])
-    for part in [*parts, latent_part, outs]:
-        part.drain()
+    for n, sent in enumerate(((sibrecv, arecv, brecv), (lsib, larecv, lbrecv))):
+        for ref, sem in zip(sent, (sib_s, a_s, b_s)):
+            wait_bytes(ref, sem.at[n])
+    outs.drain()
     for c in range(N_PART):
         store_context(c).wait()
     store_attention.wait()
@@ -528,6 +515,7 @@
             v((COLS, LAT), BF),
             v((2, TOK, LAT), BF),
             v((2, TOK, PAIR), F32),
+            v((2, TOK, PAIR), F32),
             v((2, 8, PAIR), F32),
             v((2, 8, LAT), F32),
             v((2, 8, LAT), F32),
@@ -551,19 +539,21 @@
             v((N_CHUNK, 2, CHUNK, COLS), BF),
             v((2, 4, 128, COLS), BF),
             v((4, 128, COLS), BF),
-            v((3, 128, COLS), BF),
-            dma((25,)),
+            v((2, 64, COLS), BF),
+            v((2, 128, COLS), BF),
+            v((2, 128, COLS), BF),
+            dma((20,)),
             dma((1,)),
             dma((N_PAIR,)),
             *[dma((4,))] * 2,
             *[dma((2,))] * 2,
-            *[dma((N_PART + 1,))] * 2,
-            *[dma((N_PART, 2))] * 4,
-            *[dma((1,))] * 2,
+            dma((2,)),
+            dma((N_PART + 1,)),
+            *[dma((2,)), dma((N_PART + 1, 2))] * 2,
             dma((N_PART + 2,)),
         ],
         compiler_params=pltpu.CompilerParams(
-            collective_id=0, has_side_effects=True, vmem_limit_bytes=50 * 1024 * 1024
+            collective_id=0, has_side_effects=True, vmem_limit_bytes=52 * 1024 * 1024
         ),
         cost_estimate=pl.CostEstimate(flops=13_000_000_000, bytes_accessed=20_000_000, transcendentals=4_200_000),
     )(

time: 58.4 us -> 57.2 us (0.979); the launches traced: 58.3 us -> 56.2 us
  Pallas kernels: 55.6 us -> 53.5 us
    pallas_call x1, Pallas kernels: 55.6 us -> 53.5 us  [body(): pl.pallas_call(kernel, out_shape=(jax.ShapeDtypeStruct((LAT // N_SEQ, COL...]
where the time goes in v4:
time: 57.2 us; the launch traced here: 56.2 us
  Pallas kernels  53.5 us (94%)
  local copies, waits for them, and re-layouts  2.05 us (4%)
  between operations  0.64 us (1%)
    pallas_call x1, Pallas kernels, body(): pl.pallas_call(kernel, out_shape=(jax.ShapeDtypeStruct((LAT // N_SEQ, COL...  53.5 us
    unnamed x3, local copies, waits for them, and re-layouts  2.05 us

profile of v4, /device:TPU:0, one launch (start us, length us, event | category | flops | bytes accessed | tf_op | source)
XLA Modules:
  0.0 56.2 jit_solution(6705093194599164785)
XLA Ops:
  0.6 53.5 %shard_map.94 = (bf16[128,256]{1,0:T(8,128)(2,1)S(1)}, bf16[128,256]{1,0:T(8,128)(2,1)S(1)}, bf16[1024,256]{1,0:T(8,128)(2,1)S(1)}) custom-call(bf16[2048,2048]{1,0:T(8,128)(2,1)} %lat_hbm.1, bf16[1024,2048]{1,0:T(8,128)(2,1)} %ctx_hbm.1, s32[8,1,256]{2,1,0:T(1,128)} %bitcast.1, bf16[2048,256]{1,0:T(8,128)(2,1)} %wq_hbm.1, bf16[2048,256]{1,0:T(8,128)(2,1)} %wk_hbm.1, ...), custom_call_target="tpu_custom_call" | custom-call | flops 12999999488 | bytes 20000000 | tf_op jit(solution)/shard_map/pallas_call | solution.py:492
  54.2 0.6 %copy.13 = bf16[128,256]{1,0:T(8,128)(2,1)} copy(bf16[128,256]{1,0:T(8,128)(2,1)S(1)} %get-tuple-element.6) | data formatting | bytes 131072
  54.8 0.6 %copy.14 = bf16[128,256]{1,0:T(8,128)(2,1)} copy(bf16[128,256]{1,0:T(8,128)(2,1)S(1)} %get-tuple-element.7) | data formatting | bytes 131072
  55.5 0.8 %copy.15 = bf16[1024,256]{1,0:T(8,128)(2,1)} copy(bf16[1024,256]{1,0:T(8,128)(2,1)S(1)} %get-tuple-element.8) | data formatting | bytes 1048576

commit v5 on v4

--- a/solution.py
+++ b/solution.py
@@ -154,9 +154,9 @@
             v1T[h, 0:E, rc] = vt[h * E : (h + 1) * E, :]
 
     load_q.wait()
-    for p in range(2):
-        load_pair(p).wait()
-        qT[:, p * PAIR : (p + 1) * PAIR] = dot(lat[p], wq[...]).astype(BF).T
+    load_pair(0).wait()
+    load_pair(1).wait()
+    qT[:, 0 : 2 * PAIR] = dot(lat[0:2].reshape(2 * PAIR, WIDE), wq[...]).astype(BF).T
     load_k.wait()
     load_v.wait()
     load_offsets.start()

time: 57.2 us -> 57.5 us (level)
  no operation moved by 1% of the time
where the time goes in v5:
time: 57.5 us; the launch traced here: 56.5 us
  Pallas kernels  53.8 us (94%)
  local copies, waits for them, and re-layouts  2.05 us (4%)
  between operations  0.64 us (1%)
    pallas_call x1, Pallas kernels, body(): pl.pallas_call(kernel, out_shape=(jax.ShapeDtypeStruct((LAT // N_SEQ, COL...  53.8 us
    unnamed x3, local copies, waits for them, and re-layouts  2.05 us

profile of v5, /device:TPU:0, one launch (start us, length us, event | category | flops | bytes accessed | tf_op | source)
XLA Modules:
  0.0 56.5 jit_solution(7539498301255228651)
XLA Ops:
  0.6 53.8 %shard_map.94 = (bf16[128,256]{1,0:T(8,128)(2,1)S(1)}, bf16[128,256]{1,0:T(8,128)(2,1)S(1)}, bf16[1024,256]{1,0:T(8,128)(2,1)S(1)}) custom-call(bf16[2048,2048]{1,0:T(8,128)(2,1)} %lat_hbm.1, bf16[1024,2048]{1,0:T(8,128)(2,1)} %ctx_hbm.1, s32[8,1,256]{2,1,0:T(1,128)} %bitcast.1, bf16[2048,256]{1,0:T(8,128)(2,1)} %wq_hbm.1, bf16[2048,256]{1,0:T(8,128)(2,1)} %wk_hbm.1, ...), custom_call_target="tpu_custom_call" | custom-call | flops 12999999488 | bytes 20000000 | tf_op jit(solution)/shard_map/pallas_call | solution.py:492
  54.4 0.6 %copy.13 = bf16[128,256]{1,0:T(8,128)(2,1)} copy(bf16[128,256]{1,0:T(8,128)(2,1)S(1)} %get-tuple-element.6) | data formatting | bytes 131072
  55.1 0.6 %copy.14 = bf16[128,256]{1,0:T(8,128)(2,1)} copy(bf16[128,256]{1,0:T(8,128)(2,1)S(1)} %get-tuple-element.7) | data formatting | bytes 131072
  55.7 0.8 %copy.15 = bf16[1024,256]{1,0:T(8,128)(2,1)} copy(bf16[1024,256]{1,0:T(8,128)(2,1)S(1)} %get-tuple-element.8) | data formatting | bytes 1048576
